TPU v7x, 256 devices: a whole 4x4x8 slice. The times are simulated.
256 devices in a mesh: ctx: 32 (over z, y_hi, core), tp: 8 (over x, y_lo).
Axes of the slice: x: 4, y: 4 (y_hi: 2, y_lo: 2; y = y_hi * 2 + y_lo), z: 8, core: 2. Of those that a mesh axis runs over, the one named last changes fastest.
Arguments:
- hidden_states: bfloat16 [8192, 4096], P('ctx', 'tp'), may hold values from -40 to 40
- w_query: bfloat16 [4096, 4096], P(None, 'tp'), may hold values from -0.25 to 0.25
- w_key: bfloat16 [4096, 1024], P(None, 'tp'), may hold values from -0.5 to 0.5
- w_value: bfloat16 [4096, 1024], P(None, 'tp'), may hold values from -0.09375 to 0.09375
- w_out: bfloat16 [4096, 4096], P('tp'), may hold values from -0.09375 to 0.09375
- span_order: int32 [64], replicated, may hold values from 0 to 63, each once
- lengths: int32 [4], replicated, may hold values from 1 to 4096, 8192 in all
Outputs:
- attention_out: bfloat16 [8192, 4096], P('ctx', 'tp')
Inputs may be any that keep to these rules, and one draw needn't show every extreme that they name: `span_order`: each value appears exactly once. `lengths`: they sum to 8192; the longest is exactly 4096.
All inputs are finite; a program needn't handle non-finite values.
Results may differ from a plain program's by a relative error of at most 0.02.
Values may be sent and summed in bfloat16 or wider, within the bound.
No kernel may reach another device: no remote copies, remote signals or barrier semaphores. Data moves between devices by JAX's collectives and lax.ppermute only.
A program may use at most 64 MiB of HBM per device.

v0:
```python
import math

import jax
import jax.numpy as jnp
from jax import lax
from jax.experimental import pallas as pl
from jax.experimental.pallas import tpu as pltpu
from jax.sharding import PartitionSpec as P

HEADS = 32
KV_HEADS = 8
HEAD_DIM = 128
GROUP = HEADS // KV_HEADS
SPAN = 128
SEQ = 8192
D = 4096
N_CTX = 32
N_TP = 8
N_X = 4
FEATS = D // N_TP
ROWS = SEQ // N_CTX
HALF = ROWS // 2
BLOCKS = SEQ // SPAN
OWN_BLOCKS = ROWS // SPAN
STACK = GROUP * SPAN
WIDE = 8
LIST = 32

ROPE_BASE = 500000.0
MASKED = -1e30
LOWEST = -1e29
SCALE = math.log2(math.e) / math.sqrt(HEAD_DIM)

CHUNKS = [
    [(0, 0), (0, 1), (-1, 0), (-1, 1), (1, 0), (1, 1)],
    [(-2, 0), (-2, 1), (2, 0), (2, 1)],
    [(-3, 0), (-3, 1), (3, 0), (3, 1)],
    [(4, 0), (4, 1)],
]
NARROW = [4, 4, 4, 2]
FIRST_SLOT = [0]
for chunk in CHUNKS:
    FIRST_SLOT.append(FIRST_SLOT[-1] + OWN_BLOCKS * len(chunk))
SIDES = 2
QUERY_BLOCKS = SIDES * OWN_BLOCKS
N_LISTS = len(CHUNKS) * QUERY_BLOCKS


def vmem():
    return pl.BlockSpec(memory_space=pltpu.VMEM)


def smem():
    return pl.BlockSpec(memory_space=pltpu.SMEM)


def call(kernel, shapes, in_specs, out_specs=None, scratch=(), vmem_mb=32, flops=0, nbytes=0):
    many = isinstance(shapes, (list, tuple))
    if out_specs is None:
        out_specs = [vmem() for _ in shapes] if many else vmem()
    return pl.pallas_call(
        kernel,
        out_shape=shapes,
        in_specs=in_specs,
        out_specs=out_specs,
        scratch_shapes=list(scratch),
        compiler_params=pltpu.CompilerParams(vmem_limit_bytes=vmem_mb << 20),
        cost_estimate=pl.CostEstimate(flops=flops, bytes_accessed=nbytes, transcendentals=0),
    )


def struct(shape, dtype=jnp.bfloat16):
    return jax.ShapeDtypeStruct(shape, dtype)


def member(me, dx, flip):
    x, y = me // 2, me % 2
    return ((x + dx + N_X) % N_X) * 2 + (y + flip) % 2


def tp_pairs(dx, flip):
    return [(t, ((t // 2 + dx) % N_X) * 2 + ((t % 2) ^ flip)) for t in range(N_TP)]


def send(rows, dx, flip):
    return lax.ppermute(rows, "tp", tp_pairs(dx, flip))


FLIP_CORE = [(i, i ^ 1) for i in range(N_CTX)]
FLIP_Y = [(i, i ^ 2) for i in range(N_CTX)]
UP_Z = [(i, (i + 4) % N_CTX) for i in range(N_CTX)]
DOWN_Z = [(i, (i - 4) % N_CTX) for i in range(N_CTX)]


def start_of(bounds, position):
    start = jnp.int32(0)
    for bound in bounds:
        start = jnp.where(bound <= position, bound, start)
    return start


def plan_kernel(span_ref, len_ref, ctx_ref, slot_out, pos_out, meta_out, slot_sc, count_sc):
    ctx = ctx_ref[0]
    z, y, core = ctx // 4, (ctx // 2) % 2, ctx % 2
    for p in range(BLOCKS):
        slot_sc[p] = -1
    slot = 0
    for chunk in CHUNKS:
        for k, fy in chunk:
            source = ((z + k + 8) % 8) * 4 + ((y + fy) % 2) * 2 + core
            for h in range(OWN_BLOCKS):
                slot_sc[span_ref[source * OWN_BLOCKS + h]] = slot
                slot += 1
    one = len_ref[0]
    two = one + len_ref[1]
    three = two + len_ref[2]
    bounds = (one, two, three)
    for i in range(3):
        meta_out[2 * N_LISTS + i] = bounds[i]
    for i in range(N_LISTS):
        count_sc[i] = 0
    for b in range(QUERY_BLOCKS):
        holder = ctx if b < OWN_BLOCKS else ctx + 1 - 2 * core
        own = span_ref[holder * OWN_BLOCKS + b % OWN_BLOCKS]
        meta_out[2 * N_LISTS + 3 + b] = own
        low = start_of(bounds, own * SPAN) // SPAN
        plain = jnp.minimum((start_of(bounds, own * SPAN + SPAN - 1) + SPAN - 1) // SPAN, own)

        def add(p):
            s = slot_sc[p]

            @pl.when(s >= 0)
            def _():
                c = jnp.int32(0)
                base = jnp.int32(0)
                for first in FIRST_SLOT[1:-1]:
                    c = c + jnp.where(s >= first, 1, 0)
                    base = jnp.where(s >= first, first, base)
                which = c * QUERY_BLOCKS + b
                n = count_sc[which]
                slot_out[which * LIST + n] = s - base
                pos_out[which * LIST + n] = p
                count_sc[which] = n + 1

        def body(p, carry):
            add(p)
            return carry

        lax.fori_loop(jnp.maximum(plain, low), own, body, 0)
        for c in range(len(CHUNKS)):
            meta_out[2 * (c * QUERY_BLOCKS + b) + 1] = count_sc[c * QUERY_BLOCKS + b]
        lax.fori_loop(low, plain, body, 0)
        add(own)
        for c in range(len(CHUNKS)):
            which = c * QUERY_BLOCKS + b
            n = count_sc[which]
            meta_out[2 * which] = n
            for g in range(NARROW[c] - 1):
                slot_out[which * LIST + n + g] = 0
                pos_out[which * LIST + n + g] = BLOCKS


def rotate(values, cosine, sine):
    return values * cosine + pltpu.roll(values, HEAD_DIM // 2, 1) * sine


def rows_of(me, w_ref, dx, flip):
    return w_ref[pl.ds(pl.multiple_of(member(me, dx, flip) * FEATS, FEATS), FEATS), :]


def project_near(me, refs, w_ref):
    total = None
    for (dx, flip), ref in zip(((0, 0), (0, 1), (-1, 0), (1, 0)), refs):
        part = jnp.dot(ref[...], rows_of(me, w_ref, dx, flip), preferred_element_type=jnp.float32)
        total = part if total is None else total + part
    return total


def project_far(me, refs, w_ref):
    left, right, beside, top, low = refs
    total = None
    for (dx, flip), a, b in (
        ((-1, 1), left[:HALF, :], beside[:HALF, :]),
        ((1, 1), beside[HALF:, :], right[:HALF, :]),
        ((2, 0), left[HALF:, :], right[HALF:, :]),
        ((2, 1), top[...], low[...]),
    ):
        part = jnp.dot(
            jnp.concatenate([a, b], axis=0), rows_of(me, w_ref, dx, flip), preferred_element_type=jnp.float32
        )
        total = part if total is None else total + part
    return total


def kv_near_kernel(me_ref, a, b, c, d, w_ref, out_ref):
    out_ref[...] = project_near(me_ref[0], (a, b, c, d), w_ref)


def kv_far_kernel(me_ref, a, b, c, d, e, near_ref, w_ref, cos_ref, sin_ref, out_ref):
    total = near_ref[...] + project_far(me_ref[0], (a, b, c, d, e), w_ref)
    out_ref[:, :HEAD_DIM] = rotate(total[:, :HEAD_DIM], cos_ref[...], sin_ref[...]).astype(jnp.bfloat16)
    out_ref[:, HEAD_DIM:] = total[:, HEAD_DIM:].astype(jnp.bfloat16)


def q_kernel(me_ref, *refs):
    pieces, (w_ref, cos_ref, sin_ref, out_ref) = refs[:9], refs[9:]
    queries = project_near(me_ref[0], pieces[:4], w_ref) + project_far(me_ref[0], pieces[4:], w_ref)
    for h in range(GROUP):
        turned = rotate(queries[:, h * HEAD_DIM:(h + 1) * HEAD_DIM], cos_ref[...], sin_ref[...]).astype(jnp.bfloat16)
        for b in range(OWN_BLOCKS):
            out_ref[b, h * SPAN:(h + 1) * SPAN, :] = turned[b * SPAN:(b + 1) * SPAN, :]


def attend_kernel(index, side, slot_ref, pos_ref, meta_ref, q_ref, kv_ref, *refs):
    narrow_width = NARROW[index]
    has_wide = FIRST_SLOT[index + 1] - FIRST_SLOT[index] > WIDE
    sends = side == 1 and index == len(CHUNKS) - 1
    if index == 0:
        m_ref, acc_ref = refs
        m_ref[...] = jnp.full(m_ref.shape, LOWEST, jnp.float32)
        acc_ref[...] = jnp.zeros(acc_ref.shape, jnp.float32)
    else:
        m_ref, acc_ref = refs[-2:]
        m_ref[...] = refs[0][...]
        acc_ref[...] = refs[1][...]
    bounds = [meta_ref[2 * N_LISTS + i] for i in range(3)]

    def block(b, unused):
        which = index * QUERY_BLOCKS + side * OWN_BLOCKS + b
        own = meta_ref[2 * N_LISTS + 3 + side * OWN_BLOCKS + b]
        count, plain = meta_ref[2 * which], meta_ref[2 * which + 1]
        row_pos = own * SPAN + lax.broadcasted_iota(jnp.int32, (SPAN, 1), 0)
        row_start = jnp.zeros((SPAN, 1), jnp.int32)
        for bound in bounds:
            row_start = jnp.where(bound <= row_pos, bound, row_start)

        def step(at, width, masked):
            parts = [
                kv_ref[pl.ds(pl.multiple_of(slot_ref[at + g] * SPAN, SPAN), SPAN), :] for g in range(width)
            ]
            k = jnp.concatenate([p[:, :HEAD_DIM] for p in parts], axis=0)
            v = jnp.concatenate([p[:, HEAD_DIM:] for p in parts], axis=0)
            v = jnp.concatenate([v, jnp.ones((width * SPAN, HEAD_DIM), jnp.bfloat16)], axis=1)
            heads = [slice(h * SPAN, (h + 1) * SPAN) for h in range(GROUP)]
            scores = [
                lax.dot_general(q_ref[b, h, :], k, (((1,), (1,)), ((), ())), preferred_element_type=jnp.float32) * SCALE
                for h in heads
            ]
            if masked:
                lane = lax.broadcasted_iota(jnp.int32, (SPAN, SPAN), 1)
                key_pos = jnp.concatenate([pos_ref[at + g] * SPAN + lane for g in range(width)], axis=1)
                bias = jnp.where((key_pos <= row_pos) & (key_pos >= row_start), 0.0, MASKED)
                scores = [s + bias for s in scores]
            old = [m_ref[b, h, :] for h in heads]
            new = [jnp.maximum(o, jnp.max(s, axis=1, keepdims=True)) for o, s in zip(old, scores)]
            weights = [
                jnp.exp2(s - jnp.concatenate([n] * width, axis=1)).astype(jnp.bfloat16) for s, n in zip(scores, new)
            ]
            for h, o, n, w in zip(heads, old, new, weights):
                m_ref[b, h, :] = n
                alpha = jnp.exp2(o - n)
                acc_ref[b, h, :] = acc_ref[b, h, :] * jnp.concatenate([alpha, alpha], axis=1) + jnp.dot(
                    w, v, preferred_element_type=jnp.float32
                )

        def wide(i, carry):
            step(which * LIST + i * WIDE, WIDE, False)
            return carry

        done = plain // WIDE * WIDE if has_wide else 0

        def narrow(i, carry):
            step(which * LIST + done + i * narrow_width, narrow_width, True)
            return carry

        if has_wide:
            lax.fori_loop(0, plain // WIDE, wide, 0)
        lax.fori_loop(0, (count - done + narrow_width - 1) // narrow_width, narrow, 0)
        return unused

    lax.fori_loop(0, OWN_BLOCKS, block, 0)
    if sends:
        rows_ref, stats_ref = refs[2:4]
        for b in range(OWN_BLOCKS):
            for h in range(GROUP):
                part = slice(h * SPAN, (h + 1) * SPAN)
                g = b * GROUP + h
                total = acc_ref[b, part, HEAD_DIM:]
                mean = acc_ref[b, part, :HEAD_DIM] / jnp.where(total > 0.0, total, 1.0)
                rows_ref[b, part, :] = mean.astype(jnp.bfloat16)
                stats_ref[g:g + 1, :] = jnp.sum(jnp.where(diagonal(), m_ref[b, part, :], 0.0), axis=0, keepdims=True)
                g += QUERY_BLOCKS * GROUP // SIDES
                stats_ref[g:g + 1, :] = jnp.sum(jnp.where(diagonal(), total, 0.0), axis=0, keepdims=True)


def diagonal():
    return lax.broadcasted_iota(jnp.int32, (SPAN, SPAN), 0) == lax.broadcasted_iota(jnp.int32, (SPAN, SPAN), 1)


def merge_kernel(m_ref, acc_ref, rows_ref, stats_ref, out_ref):
    for b in range(OWN_BLOCKS):
        for h in range(GROUP):
            part = slice(h * SPAN, (h + 1) * SPAN)
            g = b * GROUP + h
            column = lambda i: jnp.sum(jnp.where(diagonal(), stats_ref[i:i + 1, :], 0.0), axis=1, keepdims=True)
            their_high, their_total = column(g), column(g + OWN_BLOCKS * GROUP)
            high = m_ref[b, part, :]
            top = jnp.maximum(high, their_high)
            mine = jnp.exp2(high - top)
            theirs = jnp.exp2(their_high - top) * their_total
            summed = acc_ref[b, part, :HEAD_DIM] * mine + rows_ref[b, part, :].astype(jnp.float32) * theirs
            total = acc_ref[b, part, HEAD_DIM:] * mine + theirs
            out_ref[b * SPAN:(b + 1) * SPAN, h * HEAD_DIM:(h + 1) * HEAD_DIM] = (summed / total).astype(jnp.bfloat16)


def share(me, ctx_ref, w_ref, dx, flip):
    col = pl.multiple_of(member(me, dx, flip) * FEATS, FEATS)
    return jnp.dot(ctx_ref[...], w_ref[:, pl.ds(col, FEATS)], preferred_element_type=jnp.float32)


def far_kernel(me_ref, ctx_ref, w_ref, top_ref, low_ref):
    total = share(me_ref[0], ctx_ref, w_ref, 2, 1).astype(jnp.bfloat16)
    top_ref[...] = total[:HALF]
    low_ref[...] = total[HALF:]


def middle_kernel(me_ref, ctx_ref, w_ref, beside_ref, left_ref, right_ref, across_ref):
    left = share(me_ref[0], ctx_ref, w_ref, -1, 1)
    right = share(me_ref[0], ctx_ref, w_ref, 1, 1)
    beside_ref[:HALF, :] = left[HALF:].astype(jnp.bfloat16)
    beside_ref[HALF:, :] = right[:HALF].astype(jnp.bfloat16)
    left_ref[...] = left[:HALF]
    right_ref[...] = right[HALF:]
    across_ref[...] = share(me_ref[0], ctx_ref, w_ref, 2, 0).astype(jnp.bfloat16)


def near_kernel(me_ref, ctx_ref, w_ref, own_ref, beside_ref, left_ref, right_ref):
    own_ref[...] = share(me_ref[0], ctx_ref, w_ref, 0, 0)
    beside_ref[...] = share(me_ref[0], ctx_ref, w_ref, 0, 1)
    left_ref[...] = share(me_ref[0], ctx_ref, w_ref, -1, 0)
    right_ref[...] = share(me_ref[0], ctx_ref, w_ref, 1, 0)


def add(a, b):
    return (a + b.astype(jnp.float32)).astype(jnp.bfloat16)


def body(hidden_states, w_query, w_key, w_value, w_out, span_order, lengths):
    own_ctx = lax.axis_index("ctx")
    me = lax.axis_index("tp").reshape(1)

    with jax.named_scope("gather_hidden"):
        beside = send(hidden_states, 0, 1)
        left, right = send(hidden_states, 1, 0), send(hidden_states, -1, 0)
        from_left = send(jnp.concatenate([beside[:HALF], left[:HALF]]), 1, 0)
        from_right = send(jnp.concatenate([beside[HALF:], right[HALF:]]), -1, 0)
        from_beside = send(jnp.concatenate([left[HALF:], right[:HALF]]), 0, 1)
        far_top = send(from_left[:HALF], 1, 0)
        far_low = send(from_right[:HALF], -1, 0)
    near = [hidden_states, beside, left, right]
    far = [from_left, from_right, from_beside, far_top, far_low]

    with jax.named_scope("tables"):
        own_spans = lax.dynamic_slice_in_dim(span_order, own_ctx * OWN_BLOCKS, OWN_BLOCKS, 0)
        positions = (own_spans[:, None] * SPAN + jnp.arange(SPAN, dtype=jnp.int32)[None, :]).reshape(ROWS)
        exponent = jnp.arange(HEAD_DIM // 2, dtype=jnp.float32) * (2.0 / HEAD_DIM)
        angles = positions.astype(jnp.float32)[:, None] * jnp.power(jnp.float32(ROPE_BASE), -exponent)[None, :]
        cosine, sine = jnp.cos(angles), jnp.sin(angles)
        cosine = jnp.concatenate([cosine, cosine], axis=1)
        sine = jnp.concatenate([-sine, sine], axis=1)
        w_kv = jnp.concatenate([w_key, w_value], axis=1)

    plan = call(
        plan_kernel,
        [
            struct((N_LISTS * LIST,), jnp.int32),
            struct((N_LISTS * LIST,), jnp.int32),
            struct((2 * N_LISTS + 3 + OWN_BLOCKS,), jnp.int32),
        ],
        [smem()] * 3,
        [smem()] * 3,
        scratch=[pltpu.SMEM((BLOCKS,), jnp.int32), pltpu.SMEM((N_LISTS,), jnp.int32)],
        nbytes=4 << 20,
    )(span_order, lengths, own_ctx.reshape(1))

    kv_near = call(
        kv_near_kernel,
        struct((ROWS, 2 * HEAD_DIM), jnp.float32),
        [smem()] + [vmem()] * 5,
        flops=2 * ROWS * D * HEAD_DIM,
        nbytes=3 << 20,
    )(me, *near, w_kv)
    kv_near, plan = lax.optimization_barrier((kv_near, plan))
    kv = call(
        kv_far_kernel,
        struct((ROWS, 2 * HEAD_DIM)),
        [smem()] + [vmem()] * 9,
        flops=2 * ROWS * D * HEAD_DIM,
        nbytes=3 << 20,
    )(me, *far, kv_near, w_kv, cosine, sine)

    queries = call(
        q_kernel,
        struct((OWN_BLOCKS, STACK, HEAD_DIM)),
        [smem()] + [vmem()] * 12,
        flops=2 * ROWS * D * GROUP * HEAD_DIM,
        nbytes=6 << 20,
    )(me, *near, *far, w_query, cosine, sine)

    state_shapes = [
        struct((OWN_BLOCKS, STACK, HEAD_DIM), jnp.float32),
        struct((OWN_BLOCKS, STACK, 2 * HEAD_DIM), jnp.float32),
    ]
    sent_shapes = [struct((OWN_BLOCKS, STACK, HEAD_DIM)), struct((2 * OWN_BLOCKS * GROUP, SPAN), jnp.float32)]

    def attend(index, side, chunk, state):
        sends = side == 1 and index == len(CHUNKS) - 1
        return call(
            lambda *refs: attend_kernel(index, side, *refs),
            sent_shapes if sends else state_shapes,
            [smem()] * 3 + [vmem()] * (2 + len(state)),
            scratch=[pltpu.VMEM(s.shape, s.dtype) for s in state_shapes] if sends else (),
            flops=2 * ROWS * GROUP * chunk.shape[0] * HEAD_DIM,
            nbytes=4 << 20,
        )(*plan, (queries, their_queries)[side], chunk, *state)

    with jax.named_scope("gather_kv"):
        tie = lax.optimization_barrier
        their_queries = lax.ppermute(queries, "ctx", FLIP_CORE)
        column = jnp.concatenate([kv, lax.ppermute(kv, "ctx", FLIP_Y)], axis=0)
        column, their_queries = tie((column, their_queries))
        up, down = lax.ppermute(column, "ctx", UP_Z), lax.ppermute(column, "ctx", DOWN_Z)
        up2, down2 = lax.ppermute(up, "ctx", UP_Z), lax.ppermute(down, "ctx", DOWN_Z)
        chunk = jnp.concatenate([column, up, down], axis=0)
        theirs, mine = attend(0, 1, chunk, ()), attend(0, 0, chunk, ())
        up2, down2, theirs, mine = tie((up2, down2, theirs, mine))
        up3, down3 = lax.ppermute(up2, "ctx", UP_Z), lax.ppermute(down2, "ctx", DOWN_Z)
        chunk = jnp.concatenate([up2, down2], axis=0)
        theirs, mine = attend(1, 1, chunk, theirs), attend(1, 0, chunk, mine)
        up3, down3, theirs, mine = tie((up3, down3, theirs, mine))
        up4, down4 = lax.ppermute(up3[:ROWS], "ctx", UP_Z), lax.ppermute(down3[ROWS:], "ctx", DOWN_Z)
        chunk = jnp.concatenate([up3, down3], axis=0)
        theirs, mine = attend(2, 1, chunk, theirs), attend(2, 0, chunk, mine)
        up4, down4, theirs, mine = tie((up4, down4, theirs, mine))
        chunk = jnp.concatenate([up4, down4], axis=0)
        theirs = [lax.ppermute(sent, "ctx", FLIP_CORE) for sent in attend(3, 1, chunk, theirs)]
        mine = attend(3, 0, chunk, mine)
        context = call(
            merge_kernel, struct((ROWS, GROUP * HEAD_DIM)), [vmem()] * 4, flops=1 << 20, nbytes=2 << 20
        )(*mine, *theirs)

    with jax.named_scope("scatter_out"):
        block = struct((ROWS, FEATS), jnp.float32)
        part = struct((HALF, FEATS), jnp.float32)
        top, low = call(
            far_kernel, [struct((HALF, FEATS))] * 2, [smem()] + [vmem()] * 2, flops=2 * ROWS * FEATS * FEATS, nbytes=1 << 20
        )(me, context, w_out)
        context, top, low = lax.optimization_barrier((context, top, low))
        from_right, from_left = send(top, -1, 0), send(low, 1, 0)
        beside, left, right, across = call(
            middle_kernel,
            [struct((ROWS, FEATS)), part, part, struct((ROWS, FEATS))],
            [smem()] + [vmem()] * 2,
            flops=6 * ROWS * FEATS * FEATS,
            nbytes=3 << 20,
        )(me, context, w_out)
        from_beside = send(beside, 0, 1)
        own, own_beside, own_left, own_right = call(
            near_kernel, [block] * 4, [smem()] + [vmem()] * 2, flops=8 * ROWS * FEATS * FEATS, nbytes=4 << 20
        )(me, context, w_out)
        second_right = send(jnp.concatenate([add(left, from_right), across[:HALF]]), -1, 0)
        second_left = send(jnp.concatenate([add(right, from_left), across[HALF:]]), 1, 0)
        own_beside = add(own_beside, jnp.concatenate([second_right[:HALF], second_left[:HALF]]))
        own_left = add(own_left, jnp.concatenate([second_right[HALF:], from_beside[:HALF]]))
        own_right = add(own_right, jnp.concatenate([from_beside[HALF:], second_left[HALF:]]))
        arrived = [send(own_beside, 0, 1), send(own_left, -1, 0), send(own_right, 1, 0)]
        for rows in arrived:
            own = own + rows.astype(jnp.float32)
        return own.astype(jnp.bfloat16)


def solution(mesh):
    in_specs = (
        P("ctx", "tp"),
        P(None, "tp"),
        P(None, "tp"),
        P(None, "tp"),
        P("tp", None),
        P(),
        P(),
    )
    return jax.shard_map(body, mesh=mesh, in_specs=in_specs, out_specs=P("ctx", "tp"), check_vma=False)
```

profile of v0, /device:TPU:48, one launch (start us, length us, event | category | flops | bytes accessed | tf_op | source)
XLA Modules:
  0.0 105.2 jit_solution(7370312834902501557)
XLA Ops:
  1.3 1.5 %collective-permute-start.1 = (bf16[256,512]{1,0:T(8,128)(2,1)}, bf16[256,512]{1,0:T(8,128)(2,1)S(1)}, u32[]{:S(2)}, u32[]{:S(2)}) collective-permute-start(bf16[256,512]{1,0:T(8,128)(2,1)} %refs_0_.1), channel_id=1, source_target_pairs={{0,2},{1,3},{2,4},{3,5},{4,6},{5,7},{6,0},{7,1},{8,10},{9,11},{10,... | collective-permute-start | bytes 786440 | tf_op jit(solution)/shard_map/gather_hidden/ppermute | solution.py:86
  2.8 1.7 %collective-permute-start.2 = (bf16[256,512]{1,0:T(8,128)(2,1)}, bf16[256,512]{1,0:T(8,128)(2,1)S(1)}, u32[]{:S(2)}, u32[]{:S(2)}) collective-permute-start(bf16[256,512]{1,0:T(8,128)(2,1)} %refs_0_.1), channel_id=1, source_target_pairs={{0,6},{1,7},{2,0},{3,1},{4,2},{5,3},{6,4},{7,5},{8,14},{9,15},{10,... | collective-permute-start | bytes 786440 | tf_op jit(solution)/shard_map/gather_hidden/ppermute | solution.py:86
  4.5 1.4 %constant_dynamic-update-slice_fusion.1 = bf16[4096,256]{1,0:T(8,128)(2,1)S(1)} fusion(bf16[4096,128]{1,0:T(8,128)(2,1)} %param.9), kind=kLoop, calls=%fused_computation.18 | loop fusion | bytes 2097152
  6.0 1.5 %constant_dynamic-update-slice_fusion.w_ref = bf16[4096,256]{1,0:T(8,128)(2,1)S(1)} fusion(bf16[4096,256]{1,0:T(8,128)(2,1)S(1)} %constant_dynamic-update-slice_fusion.1, bf16[4096,128]{1,0:T(8,128)(2,1)} %param.10), kind=kLoop, calls=%fused_computation.17 | loop fusion | bytes 2097152 | tf_op jit(solution)/shard_map/tables/concatenate | solution.py:371
  7.6 2.2 %shard_map.74 = (s32[512]{0:T(512)S(1)}, s32[512]{0:T(512)S(1)}, s32[37]{0:T(128)S(1)}) custom-call(s32[64]{0:T(128)S(1)} %copy-done.3, s32[4]{0:T(128)S(1)} %copy-done.4, s32[1]{0:T(128)} %bitcast.1.ctx_ref), custom_call_target="tpu_custom_call" | custom-call | bytes 4194304 | tf_op jit(solution)/shard_map/pallas_call | solution.py:373
  11.0 3.0 %collective-permute-start.4 = (bf16[256,512]{1,0:T(8,128)(2,1)S(1)}, bf16[256,512]{1,0:T(8,128)(2,1)S(1)}, u32[]{:S(2)}, u32[]{:S(2)}) collective-permute-start(bf16[256,512]{1,0:T(8,128)(2,1)S(1)} %pad_maximum_fusion.1), channel_id=1, source_target_pairs={{0,6},{1,7},{2,0},{3,1},{4,2},{5,3},{6,4},{7,5},{8,14},{9,15},{10,... | collective-permute-start | bytes 786440 | tf_op jit(solution)/shard_map/gather_hidden/ppermute | solution.py:86
  15.4 3.3 %collective-permute-done.3.refs_4_.a = bf16[256,512]{1,0:T(8,128)(2,1)S(1)} collective-permute-done((bf16[256,512]{1,0:T(8,128)(2,1)S(1)}, bf16[256,512]{1,0:T(8,128)(2,1)S(1)}, u32[]{:S(2)}, u32[]{:S(2)}) %collective-permute-start.3) | collective-permute-done | bytes 262176 | tf_op jit(solution)/shard_map/gather_hidden/ppermute | solution.py:86
  18.9 3.3 %collective-permute-start.7 = (bf16[128,512]{1,0:T(8,128)(2,1)S(1)}, bf16[128,512]{1,0:T(8,128)(2,1)S(1)}, u32[]{:S(2)}, u32[]{:S(2)}) collective-permute-start(bf16[128,512]{1,0:T(8,128)(2,1)S(1)} %slice.79), channel_id=1, source_target_pairs={{0,6},{1,7},{2,0},{3,1},{4,2},{5,3},{6,4},{7,5},{8,14},{9,15},{10,... | collective-permute-start | bytes 393224 | tf_op jit(solution)/shard_map/gather_hidden/ppermute | solution.py:86
  22.8 2.2 %collective-permute-done.6.refs_7_.d = bf16[128,512]{1,0:T(8,128)(2,1)S(1)} collective-permute-done((bf16[128,512]{1,0:T(8,128)(2,1)S(1)}, bf16[128,512]{1,0:T(8,128)(2,1)S(1)}, u32[]{:S(2)}, u32[]{:S(2)}) %collective-permute-start.6) | collective-permute-done | bytes 131104 | tf_op jit(solution)/shard_map/gather_hidden/ppermute | solution.py:86
  25.0 1.4 %shard_map.75.refs_3_ = bf16[2,512,128]{2,1,0:T(8,128)(2,1)S(1)} custom-call(s32[1]{0:T(128)} %bitcast.me_ref, bf16[256,512]{1,0:T(8,128)(2,1)S(1)} %copy-done.2, bf16[256,512]{1,0:T(8,128)(2,1)S(1)} %collective-permute-done.b.refs_1_, bf16[256,512]{1,0:T(8,128)(2,1)S(1)} %collective-permute-done.1.c.refs_2_, ...), custom_call_target="tpu_custom_call" | custom-call | flops 1073741824 | bytes 6291456 | tf_op jit(solution)/shard_map/pallas_call | solution.py:402
  27.7 6.8 %collective-permute-done.8 = bf16[256,256]{1,0:T(8,128)(2,1)S(1)} collective-permute-done((bf16[256,256]{1,0:T(8,128)(2,1)S(1)}, bf16[256,256]{1,0:T(8,128)(2,1)S(1)}, u32[]{:S(2)}, u32[]{:S(2)}) %collective-permute-start.8) | collective-permute-done | bytes 131104 | tf_op jit(solution)/shard_map/gather_kv/ppermute | solution.py:430
  34.5 2.0 %collective-permute-start.10 = (bf16[512,256]{1,0:T(8,128)(2,1)S(1)}, bf16[512,256]{1,0:T(8,128)(2,1)S(1)}, u32[]{:S(2)}, u32[]{:S(2)}) collective-permute-start(bf16[512,256]{1,0:T(8,128)(2,1)S(1)} %pad_maximum_fusion.3), channel_id=1, source_target_pairs={{0,32},{8,40},{16,48},{24,56},{32,64},{40,72},{48,80},{56,88},{64,... | collective-permute-start | bytes 786440 | tf_op jit(solution)/shard_map/gather_kv/ppermute | solution.py:432
  36.6 5.9 %collective-permute-done.10 = bf16[512,256]{1,0:T(8,128)(2,1)S(1)} collective-permute-done((bf16[512,256]{1,0:T(8,128)(2,1)S(1)}, bf16[512,256]{1,0:T(8,128)(2,1)S(1)}, u32[]{:S(2)}, u32[]{:S(2)}) %collective-permute-start.10) | collective-permute-done | bytes 262176 | tf_op jit(solution)/shard_map/gather_kv/ppermute | solution.py:432
  42.5 1.9 %collective-permute-start.11 = (bf16[512,256]{1,0:T(8,128)(2,1)S(1)}, bf16[512,256]{1,0:T(8,128)(2,1)S(1)}, u32[]{:S(2)}, u32[]{:S(2)}) collective-permute-start(bf16[512,256]{1,0:T(8,128)(2,1)S(1)} %collective-permute-done.10), channel_id=1, source_target_pairs={{0,32},{8,40},{16,48},{24,56},{32,64},{40,72},{48,80},{56,88},{64,... | collective-permute-start | bytes 786440 | tf_op jit(solution)/shard_map/gather_kv/ppermute | solution.py:433
  44.4 2.3 %collective-permute-start.13 = (bf16[512,256]{1,0:T(8,128)(2,1)S(1)}, bf16[512,256]{1,0:T(8,128)(2,1)S(1)}, u32[]{:S(2)}, u32[]{:S(2)}) collective-permute-start(bf16[512,256]{1,0:T(8,128)(2,1)S(1)} %collective-permute-done.12), channel_id=1, source_target_pairs={{0,224},{8,232},{16,240},{24,248},{32,0},{40,8},{48,16},{56,24},{6... | collective-permute-start | bytes 786440 | tf_op jit(solution)/shard_map/gather_kv/ppermute | solution.py:433
  46.8 2.0 %gather_kv.10 = (f32[2,512,128]{2,1,0:T(8,128)S(1)}, f32[2,512,256]{2,1,0:T(8,128)S(1)}) custom-call(s32[512]{0:T(512)S(1)} %get-tuple-element.64.refs_0_, s32[512]{0:T(512)S(1)} %get-tuple-element.65.refs_1_, s32[37]{0:T(128)S(1)} %get-tuple-element.66.refs_2_, bf16[2,512,128]{2,1,0:T(8,128)(2,1)S(1)} %shard_map.75.refs_3_, ...), custom_call_target="tpu_custom_call" | custom-call | flops 402653184 | bytes 4194304 | tf_op jit(solution)/shard_map/gather_kv/pallas_call | solution.py:418
  48.8 1.4 %gather_kv.9 = (f32[2,512,128]{2,1,0:T(8,128)S(1)}, f32[2,512,256]{2,1,0:T(8,128)S(1)}) custom-call(s32[512]{0:T(512)S(1)} %get-tuple-element.64.refs_0_, s32[512]{0:T(512)S(1)} %get-tuple-element.65.refs_1_, s32[37]{0:T(128)S(1)} %get-tuple-element.66.refs_2_, bf16[2,512,128]{2,1,0:T(8,128)(2,1)S(1)} %collective-permute-done.9.refs_3_, ...), custom_call_target="tpu_custom_call" | custom-call | flops 402653184 | bytes 4194304 | tf_op jit(solution)/shard_map/gather_kv/pallas_call | solution.py:418
  50.2 2.1 %collective-permute-done.11 = bf16[512,256]{1,0:T(8,128)(2,1)S(1)} collective-permute-done((bf16[512,256]{1,0:T(8,128)(2,1)S(1)}, bf16[512,256]{1,0:T(8,128)(2,1)S(1)}, u32[]{:S(2)}, u32[]{:S(2)}) %collective-permute-start.11) | collective-permute-done | bytes 262176 | tf_op jit(solution)/shard_map/gather_kv/ppermute | solution.py:433
  52.7 3.0 %collective-permute-start.14 = (bf16[512,256]{1,0:T(8,128)(2,1)S(1)}, bf16[512,256]{1,0:T(8,128)(2,1)S(1)}, u32[]{:S(2)}, u32[]{:S(2)}) collective-permute-start(bf16[512,256]{1,0:T(8,128)(2,1)S(1)} %collective-permute-done.11), channel_id=1, source_target_pairs={{0,32},{8,40},{16,48},{24,56},{32,64},{40,72},{48,80},{56,88},{64,... | collective-permute-start | bytes 786440 | tf_op jit(solution)/shard_map/gather_kv/ppermute | solution.py:437
  58.5 1.9 %collective-permute-done.14 = bf16[512,256]{1,0:T(8,128)(2,1)S(1)} collective-permute-done((bf16[512,256]{1,0:T(8,128)(2,1)S(1)}, bf16[512,256]{1,0:T(8,128)(2,1)S(1)}, u32[]{:S(2)}, u32[]{:S(2)}) %collective-permute-start.14) | collective-permute-done | bytes 262176 | tf_op jit(solution)/shard_map/gather_kv/ppermute | solution.py:437
  60.4 2.6 %collective-permute-done.15 = bf16[512,256]{1,0:T(8,128)(2,1)S(1)} collective-permute-done((bf16[512,256]{1,0:T(8,128)(2,1)S(1)}, bf16[512,256]{1,0:T(8,128)(2,1)S(1)}, u32[]{:S(2)}, u32[]{:S(2)}) %collective-permute-start.15) | collective-permute-done | bytes 262176 | tf_op jit(solution)/shard_map/gather_kv/ppermute | solution.py:437
  63.0 2.1 %collective-permute-start.16 = (bf16[256,256]{1,0:T(8,128)(2,1)S(1)}, bf16[256,256]{1,0:T(8,128)(2,1)S(1)}, u32[]{:S(2)}, u32[]{:S(2)}) collective-permute-start(bf16[256,256]{1,0:T(8,128)(2,1)S(1)} %slice.62), channel_id=1, source_target_pairs={{0,32},{8,40},{16,48},{24,56},{32,64},{40,72},{48,80},{56,88},{64,... | collective-permute-start | bytes 393224 | tf_op jit(solution)/shard_map/gather_kv/ppermute | solution.py:441
  68.1 2.1 %collective-permute-done.17 = bf16[256,256]{1,0:T(8,128)(2,1)S(1)} collective-permute-done((bf16[256,256]{1,0:T(8,128)(2,1)S(1)}, bf16[256,256]{1,0:T(8,128)(2,1)S(1)}, u32[]{:S(2)}, u32[]{:S(2)}) %collective-permute-start.17) | collective-permute-done | bytes 131104 | tf_op jit(solution)/shard_map/gather_kv/ppermute | solution.py:441
  70.2 1.4 %gather_kv.16 = (bf16[2,512,128]{2,1,0:T(8,128)(2,1)S(1)}, f32[16,128]{1,0:T(8,128)S(1)}) custom-call(s32[512]{0:T(512)S(1)} %get-tuple-element.64.refs_0_, s32[512]{0:T(512)S(1)} %get-tuple-element.65.refs_1_, s32[37]{0:T(128)S(1)} %get-tuple-element.66.refs_2_, bf16[2,512,128]{2,1,0:T(8,128)(2,1)S(1)} %collective-permute-done.9.refs_3_, ...), custom_call_target="tpu_custom_call" | custom-call | flops 134217728 | bytes 4194304 | tf_op jit(solution)/shard_map/gather_kv/pallas_call | solution.py:418
  74.8 3.4 %collective-permute-start.20 = (bf16[128,512]{1,0:T(8,128)(2,1)S(1)}, bf16[128,512]{1,0:T(8,128)(2,1)S(1)}, u32[]{:S(2)}, u32[]{:S(2)}) collective-permute-start(bf16[128,512]{1,0:T(8,128)(2,1)S(1)} %get-tuple-element.110), channel_id=1, source_target_pairs={{0,6},{1,7},{2,0},{3,1},{4,2},{5,3},{6,4},{7,5},{8,14},{9,15},{10,... | collective-permute-start | bytes 393224 | tf_op jit(solution)/shard_map/scatter_out/ppermute | solution.py:86
  79.9 2.1 %collective-permute-done.20 = bf16[128,512]{1,0:T(8,128)(2,1)S(1)} collective-permute-done((bf16[128,512]{1,0:T(8,128)(2,1)S(1)}, bf16[128,512]{1,0:T(8,128)(2,1)S(1)}, u32[]{:S(2)}, u32[]{:S(2)}) %collective-permute-start.20) | collective-permute-done | bytes 131104 | tf_op jit(solution)/shard_map/scatter_out/ppermute | solution.py:86
  82.0 3.8 %collective-permute-start.21 = (bf16[256,512]{1,0:T(8,128)(2,1)S(1)}, bf16[256,512]{1,0:T(8,128)(2,1)S(1)}, u32[]{:S(2)}, u32[]{:S(2)}) collective-permute-start(bf16[256,512]{1,0:T(8,128)(2,1)S(1)} %pad_maximum_fusion.4), channel_id=1, source_target_pairs={{0,6},{1,7},{2,0},{3,1},{4,2},{5,3},{6,4},{7,5},{8,14},{9,15},{10,... | collective-permute-start | bytes 786440 | tf_op jit(solution)/shard_map/scatter_out/ppermute | solution.py:86
  87.2 4.3 %collective-permute-done.21 = bf16[256,512]{1,0:T(8,128)(2,1)S(1)} collective-permute-done((bf16[256,512]{1,0:T(8,128)(2,1)S(1)}, bf16[256,512]{1,0:T(8,128)(2,1)S(1)}, u32[]{:S(2)}, u32[]{:S(2)}) %collective-permute-start.21) | collective-permute-done | bytes 262176 | tf_op jit(solution)/shard_map/scatter_out/ppermute | solution.py:86
  91.5 3.5 %collective-permute-done.23 = bf16[256,512]{1,0:T(8,128)(2,1)S(1)} collective-permute-done((bf16[256,512]{1,0:T(8,128)(2,1)S(1)}, bf16[256,512]{1,0:T(8,128)(2,1)S(1)}, u32[]{:S(2)}, u32[]{:S(2)}) %collective-permute-start.23) | collective-permute-done | bytes 262176 | tf_op jit(solution)/shard_map/scatter_out/ppermute | solution.py:86
  96.3 1.9 %collective-permute-start.27 = (bf16[256,512]{1,0:T(8,128)(2,1)S(1)}, bf16[256,512]{1,0:T(8,128)(2,1)S(1)}, u32[]{:S(2)}, u32[]{:S(2)}) collective-permute-start(bf16[256,512]{1,0:T(8,128)(2,1)S(1)} %add_convert_fusion.1), channel_id=1, source_target_pairs={{0,2},{1,3},{2,4},{3,5},{4,6},{5,7},{6,0},{7,1},{8,10},{9,11},{10,... | collective-permute-start | bytes 786440 | tf_op jit(solution)/shard_map/scatter_out/ppermute | solution.py:86
  98.3 3.9 %collective-permute-done.24 = bf16[256,512]{1,0:T(8,128)(2,1)S(1)} collective-permute-done((bf16[256,512]{1,0:T(8,128)(2,1)S(1)}, bf16[256,512]{1,0:T(8,128)(2,1)S(1)}, u32[]{:S(2)}, u32[]{:S(2)}) %collective-permute-start.24) | collective-permute-done | bytes 262176 | tf_op jit(solution)/shard_map/scatter_out/ppermute | solution.py:86
  102.8 1.6 %collective-permute-done.27 = bf16[256,512]{1,0:T(8,128)(2,1)S(1)} collective-permute-done((bf16[256,512]{1,0:T(8,128)(2,1)S(1)}, bf16[256,512]{1,0:T(8,128)(2,1)S(1)}, u32[]{:S(2)}, u32[]{:S(2)}) %collective-permute-start.27) | collective-permute-done | bytes 262176 | tf_op jit(solution)/shard_map/scatter_out/ppermute | solution.py:86
  (89 shorter events, 21.3 us)
Async XLA Ops:
  0.0 5.9 %copy-start.3 = (s32[64]{0:T(128)S(1)}, s32[64]{0:T(128)}, u32[]{:S(2)}) copy-start(s32[64]{0:T(128)} %span_ref.1) | copy-start | bytes 772
  0.0 10.5 %collective-permute-start = (bf16[256,512]{1,0:T(8,128)(2,1)}, bf16[256,512]{1,0:T(8,128)(2,1)S(1)}, u32[]{:S(2)}, u32[]{:S(2)}) collective-permute-start(bf16[256,512]{1,0:T(8,128)(2,1)} %refs_0_.1), channel_id=1, source_target_pairs={{0,1},{1,0},{2,3},{3,2},{4,5},{5,4},{6,7},{7,6},{8,9},{9,8},{10,11... | collective-permute-start | bytes 786440 | tf_op jit(solution)/shard_map/gather_hidden/ppermute | solution.py:86
  1.3 9.2 %collective-permute-start.1 = (bf16[256,512]{1,0:T(8,128)(2,1)}, bf16[256,512]{1,0:T(8,128)(2,1)S(1)}, u32[]{:S(2)}, u32[]{:S(2)}) collective-permute-start(bf16[256,512]{1,0:T(8,128)(2,1)} %refs_0_.1), channel_id=1, source_target_pairs={{0,2},{1,3},{2,4},{3,5},{4,6},{5,7},{6,0},{7,1},{8,10},{9,11},{10,... | collective-permute-start | bytes 786440 | tf_op jit(solution)/shard_map/gather_hidden/ppermute | solution.py:86
  2.8 8.2 %collective-permute-start.2 = (bf16[256,512]{1,0:T(8,128)(2,1)}, bf16[256,512]{1,0:T(8,128)(2,1)S(1)}, u32[]{:S(2)}, u32[]{:S(2)}) collective-permute-start(bf16[256,512]{1,0:T(8,128)(2,1)} %refs_0_.1), channel_id=1, source_target_pairs={{0,6},{1,7},{2,0},{3,1},{4,2},{5,3},{6,4},{7,5},{8,14},{9,15},{10,... | collective-permute-start | bytes 786440 | tf_op jit(solution)/shard_map/gather_hidden/ppermute | solution.py:86
  4.5 3.1 %copy-start.4 = (s32[4]{0:T(128)S(1)}, s32[4]{0:T(128)}, u32[]{:S(2)}) copy-start(s32[4]{0:T(128)} %len_ref.1) | copy-start | bytes 52
  10.5 11.8 %copy-start.2 = (bf16[256,512]{1,0:T(8,128)(2,1)S(1)}, bf16[256,512]{1,0:T(8,128)(2,1)}, u32[]{:S(2)}) copy-start(bf16[256,512]{1,0:T(8,128)(2,1)} %refs_0_.1) | copy-start | bytes 786436
  10.6 8.1 %collective-permute-start.3 = (bf16[256,512]{1,0:T(8,128)(2,1)S(1)}, bf16[256,512]{1,0:T(8,128)(2,1)S(1)}, u32[]{:S(2)}, u32[]{:S(2)}) collective-permute-start(bf16[256,512]{1,0:T(8,128)(2,1)S(1)} %pad_maximum_fusion), channel_id=1, source_target_pairs={{0,2},{1,3},{2,4},{3,5},{4,6},{5,7},{6,0},{7,1},{8,10},{9,11},{10,... | collective-permute-start | bytes 786440 | tf_op jit(solution)/shard_map/gather_hidden/ppermute | solution.py:86
  11.0 7.8 %collective-permute-start.4 = (bf16[256,512]{1,0:T(8,128)(2,1)S(1)}, bf16[256,512]{1,0:T(8,128)(2,1)S(1)}, u32[]{:S(2)}, u32[]{:S(2)}) collective-permute-start(bf16[256,512]{1,0:T(8,128)(2,1)S(1)} %pad_maximum_fusion.1), channel_id=1, source_target_pairs={{0,6},{1,7},{2,0},{3,1},{4,2},{5,3},{6,4},{7,5},{8,14},{9,15},{10,... | collective-permute-start | bytes 786440 | tf_op jit(solution)/shard_map/gather_hidden/ppermute | solution.py:86
  14.0 8.7 %collective-permute-start.5 = (bf16[256,512]{1,0:T(8,128)(2,1)S(1)}, bf16[256,512]{1,0:T(8,128)(2,1)S(1)}, u32[]{:S(2)}, u32[]{:S(2)}) collective-permute-start(bf16[256,512]{1,0:T(8,128)(2,1)S(1)} %pad_maximum_fusion.2), channel_id=1, source_target_pairs={{0,1},{1,0},{2,3},{3,2},{4,5},{5,4},{6,7},{7,6},{8,9},{9,8},{10,11... | collective-permute-start | bytes 786440 | tf_op jit(solution)/shard_map/gather_hidden/ppermute | solution.py:86
  18.7 6.3 %collective-permute-start.6 = (bf16[128,512]{1,0:T(8,128)(2,1)S(1)}, bf16[128,512]{1,0:T(8,128)(2,1)S(1)}, u32[]{:S(2)}, u32[]{:S(2)}) collective-permute-start(bf16[128,512]{1,0:T(8,128)(2,1)S(1)} %slice.78), channel_id=1, source_target_pairs={{0,2},{1,3},{2,4},{3,5},{4,6},{5,7},{6,0},{7,1},{8,10},{9,11},{10,... | collective-permute-start | bytes 393224 | tf_op jit(solution)/shard_map/gather_hidden/ppermute | solution.py:86
  18.8 6.2 %copy-start.1 = (bf16[4096,512]{1,0:T(8,128)(2,1)S(1)}, bf16[4096,512]{1,0:T(8,128)(2,1)}, u32[]{:S(2)}) copy-start(bf16[4096,512]{1,0:T(8,128)(2,1)} %refs_9_.1) | copy-start | bytes 12582916
  18.9 6.1 %collective-permute-start.7 = (bf16[128,512]{1,0:T(8,128)(2,1)S(1)}, bf16[128,512]{1,0:T(8,128)(2,1)S(1)}, u32[]{:S(2)}, u32[]{:S(2)}) collective-permute-start(bf16[128,512]{1,0:T(8,128)(2,1)S(1)} %slice.79), channel_id=1, source_target_pairs={{0,6},{1,7},{2,0},{3,1},{4,2},{5,3},{6,4},{7,5},{8,14},{9,15},{10,... | collective-permute-start | bytes 393224 | tf_op jit(solution)/shard_map/gather_hidden/ppermute | solution.py:86
  26.4 8.1 %collective-permute-start.9 = (bf16[2,512,128]{2,1,0:T(8,128)(2,1)S(1)}, bf16[2,512,128]{2,1,0:T(8,128)(2,1)S(1)}, u32[]{:S(2)}, u32[]{:S(2)}) collective-permute-start(bf16[2,512,128]{2,1,0:T(8,128)(2,1)S(1)} %shard_map.75.refs_3_), channel_id=1, source_target_pairs={{0,8},{8,0},{16,24},{24,16},{32,40},{40,32},{48,56},{56,48},{64,72... | collective-permute-start | bytes 786440 | tf_op jit(solution)/shard_map/gather_kv/ppermute | solution.py:429
  27.0 7.5 %collective-permute-start.8 = (bf16[256,256]{1,0:T(8,128)(2,1)S(1)}, bf16[256,256]{1,0:T(8,128)(2,1)S(1)}, u32[]{:S(2)}, u32[]{:S(2)}) collective-permute-start(bf16[256,256]{1,0:T(8,128)(2,1)S(1)} %shard_map.76), channel_id=1, source_target_pairs={{0,16},{8,24},{16,0},{24,8},{32,48},{40,56},{48,32},{56,40},{64,80... | collective-permute-start | bytes 393224 | tf_op jit(solution)/shard_map/gather_kv/ppermute | solution.py:430
  34.5 8.0 %collective-permute-start.10 = (bf16[512,256]{1,0:T(8,128)(2,1)S(1)}, bf16[512,256]{1,0:T(8,128)(2,1)S(1)}, u32[]{:S(2)}, u32[]{:S(2)}) collective-permute-start(bf16[512,256]{1,0:T(8,128)(2,1)S(1)} %pad_maximum_fusion.3), channel_id=1, source_target_pairs={{0,32},{8,40},{16,48},{24,56},{32,64},{40,72},{48,80},{56,88},{64,... | collective-permute-start | bytes 786440 | tf_op jit(solution)/shard_map/gather_kv/ppermute | solution.py:432
  36.5 7.9 %collective-permute-start.12 = (bf16[512,256]{1,0:T(8,128)(2,1)S(1)}, bf16[512,256]{1,0:T(8,128)(2,1)S(1)}, u32[]{:S(2)}, u32[]{:S(2)}) collective-permute-start(bf16[512,256]{1,0:T(8,128)(2,1)S(1)} %pad_maximum_fusion.3), channel_id=1, source_target_pairs={{0,224},{8,232},{16,240},{24,248},{32,0},{40,8},{48,16},{56,24},{6... | collective-permute-start | bytes 786440 | tf_op jit(solution)/shard_map/gather_kv/ppermute | solution.py:432
  42.5 9.8 %collective-permute-start.11 = (bf16[512,256]{1,0:T(8,128)(2,1)S(1)}, bf16[512,256]{1,0:T(8,128)(2,1)S(1)}, u32[]{:S(2)}, u32[]{:S(2)}) collective-permute-start(bf16[512,256]{1,0:T(8,128)(2,1)S(1)} %collective-permute-done.10), channel_id=1, source_target_pairs={{0,32},{8,40},{16,48},{24,56},{32,64},{40,72},{48,80},{56,88},{64,... | collective-permute-start | bytes 786440 | tf_op jit(solution)/shard_map/gather_kv/ppermute | solution.py:433
  44.4 8.3 %collective-permute-start.13 = (bf16[512,256]{1,0:T(8,128)(2,1)S(1)}, bf16[512,256]{1,0:T(8,128)(2,1)S(1)}, u32[]{:S(2)}, u32[]{:S(2)}) collective-permute-start(bf16[512,256]{1,0:T(8,128)(2,1)S(1)} %collective-permute-done.12), channel_id=1, source_target_pairs={{0,224},{8,232},{16,240},{24,248},{32,0},{40,8},{48,16},{56,24},{6... | collective-permute-start | bytes 786440 | tf_op jit(solution)/shard_map/gather_kv/ppermute | solution.py:433
  52.7 7.7 %collective-permute-start.14 = (bf16[512,256]{1,0:T(8,128)(2,1)S(1)}, bf16[512,256]{1,0:T(8,128)(2,1)S(1)}, u32[]{:S(2)}, u32[]{:S(2)}) collective-permute-start(bf16[512,256]{1,0:T(8,128)(2,1)S(1)} %collective-permute-done.11), channel_id=1, source_target_pairs={{0,32},{8,40},{16,48},{24,56},{32,64},{40,72},{48,80},{56,88},{64,... | collective-permute-start | bytes 786440 | tf_op jit(solution)/shard_map/gather_kv/ppermute | solution.py:437
  55.7 7.3 %collective-permute-start.15 = (bf16[512,256]{1,0:T(8,128)(2,1)S(1)}, bf16[512,256]{1,0:T(8,128)(2,1)S(1)}, u32[]{:S(2)}, u32[]{:S(2)}) collective-permute-start(bf16[512,256]{1,0:T(8,128)(2,1)S(1)} %collective-permute-done.13), channel_id=1, source_target_pairs={{0,224},{8,232},{16,240},{24,248},{32,0},{40,8},{48,16},{56,24},{6... | collective-permute-start | bytes 786440 | tf_op jit(solution)/shard_map/gather_kv/ppermute | solution.py:437
  63.0 5.0 %collective-permute-start.16 = (bf16[256,256]{1,0:T(8,128)(2,1)S(1)}, bf16[256,256]{1,0:T(8,128)(2,1)S(1)}, u32[]{:S(2)}, u32[]{:S(2)}) collective-permute-start(bf16[256,256]{1,0:T(8,128)(2,1)S(1)} %slice.62), channel_id=1, source_target_pairs={{0,32},{8,40},{16,48},{24,56},{32,64},{40,72},{48,80},{56,88},{64,... | collective-permute-start | bytes 393224 | tf_op jit(solution)/shard_map/gather_kv/ppermute | solution.py:441
  65.1 5.0 %collective-permute-start.17 = (bf16[256,256]{1,0:T(8,128)(2,1)S(1)}, bf16[256,256]{1,0:T(8,128)(2,1)S(1)}, u32[]{:S(2)}, u32[]{:S(2)}) collective-permute-start(bf16[256,256]{1,0:T(8,128)(2,1)S(1)} %slice.63), channel_id=1, source_target_pairs={{0,224},{8,232},{16,240},{24,248},{32,0},{40,8},{48,16},{56,24},{6... | collective-permute-start | bytes 393224 | tf_op jit(solution)/shard_map/gather_kv/ppermute | solution.py:441
  71.6 1.9 %collective-permute-start.18 = (bf16[2,512,128]{2,1,0:T(8,128)(2,1)S(1)}, bf16[2,512,128]{2,1,0:T(8,128)(2,1)S(1)}, u32[]{:S(2)}, u32[]{:S(2)}) collective-permute-start(bf16[2,512,128]{2,1,0:T(8,128)(2,1)S(1)} %get-tuple-element.102), channel_id=1, source_target_pairs={{0,8},{8,0},{16,24},{24,16},{32,40},{40,32},{48,56},{56,48},{64,72... | collective-permute-start | bytes 786440 | tf_op jit(solution)/shard_map/gather_kv/ppermute | solution.py:446
  71.7 1.7 %collective-permute-start.19 = (f32[16,128]{1,0:T(8,128)S(1)}, f32[16,128]{1,0:T(8,128)S(1)}, u32[]{:S(2)}, u32[]{:S(2)}) collective-permute-start(f32[16,128]{1,0:T(8,128)S(1)} %get-tuple-element.103), channel_id=1, source_target_pairs={{0,8},{8,0},{16,24},{24,16},{32,40},{40,32},{48,56},{56,48},{64,72... | collective-permute-start | bytes 24584 | tf_op jit(solution)/shard_map/gather_kv/ppermute | solution.py:446
  74.8 7.1 %collective-permute-start.20 = (bf16[128,512]{1,0:T(8,128)(2,1)S(1)}, bf16[128,512]{1,0:T(8,128)(2,1)S(1)}, u32[]{:S(2)}, u32[]{:S(2)}) collective-permute-start(bf16[128,512]{1,0:T(8,128)(2,1)S(1)} %get-tuple-element.110), channel_id=1, source_target_pairs={{0,6},{1,7},{2,0},{3,1},{4,2},{5,3},{6,4},{7,5},{8,14},{9,15},{10,... | collective-permute-start | bytes 393224 | tf_op jit(solution)/shard_map/scatter_out/ppermute | solution.py:86
  78.2 7.5 %collective-permute-start.22 = (bf16[128,512]{1,0:T(8,128)(2,1)S(1)}, bf16[128,512]{1,0:T(8,128)(2,1)S(1)}, u32[]{:S(2)}, u32[]{:S(2)}) collective-permute-start(bf16[128,512]{1,0:T(8,128)(2,1)S(1)} %get-tuple-element.113), channel_id=1, source_target_pairs={{0,2},{1,3},{2,4},{3,5},{4,6},{5,7},{6,0},{7,1},{8,10},{9,11},{10,... | collective-permute-start | bytes 393224 | tf_op jit(solution)/shard_map/scatter_out/ppermute | solution.py:86
  78.3 8.8 %collective-permute-start.25 = (bf16[256,512]{1,0:T(8,128)(2,1)S(1)}, bf16[256,512]{1,0:T(8,128)(2,1)S(1)}, u32[]{:S(2)}, u32[]{:S(2)}) collective-permute-start(bf16[256,512]{1,0:T(8,128)(2,1)S(1)} %get-tuple-element.115), channel_id=1, source_target_pairs={{0,1},{1,0},{2,3},{3,2},{4,5},{5,4},{6,7},{7,6},{8,9},{9,8},{10,11... | collective-permute-start | bytes 786440 | tf_op jit(solution)/shard_map/scatter_out/ppermute | solution.py:86
  82.0 9.4 %collective-permute-start.21 = (bf16[256,512]{1,0:T(8,128)(2,1)S(1)}, bf16[256,512]{1,0:T(8,128)(2,1)S(1)}, u32[]{:S(2)}, u32[]{:S(2)}) collective-permute-start(bf16[256,512]{1,0:T(8,128)(2,1)S(1)} %pad_maximum_fusion.4), channel_id=1, source_target_pairs={{0,6},{1,7},{2,0},{3,1},{4,2},{5,3},{6,4},{7,5},{8,14},{9,15},{10,... | collective-permute-start | bytes 786440 | tf_op jit(solution)/shard_map/scatter_out/ppermute | solution.py:86
  85.8 9.2 %collective-permute-start.23 = (bf16[256,512]{1,0:T(8,128)(2,1)S(1)}, bf16[256,512]{1,0:T(8,128)(2,1)S(1)}, u32[]{:S(2)}, u32[]{:S(2)}) collective-permute-start(bf16[256,512]{1,0:T(8,128)(2,1)S(1)} %pad_maximum_fusion.5), channel_id=1, source_target_pairs={{0,2},{1,3},{2,4},{3,5},{4,6},{5,7},{6,0},{7,1},{8,10},{9,11},{10,... | collective-permute-start | bytes 786440 | tf_op jit(solution)/shard_map/scatter_out/ppermute | solution.py:86
  95.1 7.1 %collective-permute-start.24 = (bf16[256,512]{1,0:T(8,128)(2,1)S(1)}, bf16[256,512]{1,0:T(8,128)(2,1)S(1)}, u32[]{:S(2)}, u32[]{:S(2)}) collective-permute-start(bf16[256,512]{1,0:T(8,128)(2,1)S(1)} %add_convert_fusion.3), channel_id=1, source_target_pairs={{0,1},{1,0},{2,3},{3,2},{4,5},{5,4},{6,7},{7,6},{8,9},{9,8},{10,11... | collective-permute-start | bytes 786440 | tf_op jit(solution)/shard_map/scatter_out/ppermute | solution.py:86
  96.0 6.8 %collective-permute-start.26 = (bf16[256,512]{1,0:T(8,128)(2,1)S(1)}, bf16[256,512]{1,0:T(8,128)(2,1)S(1)}, u32[]{:S(2)}, u32[]{:S(2)}) collective-permute-start(bf16[256,512]{1,0:T(8,128)(2,1)S(1)} %add_convert_fusion.2), channel_id=1, source_target_pairs={{0,6},{1,7},{2,0},{3,1},{4,2},{5,3},{6,4},{7,5},{8,14},{9,15},{10,... | collective-permute-start | bytes 786440 | tf_op jit(solution)/shard_map/scatter_out/ppermute | solution.py:86
  96.3 8.0 %collective-permute-start.27 = (bf16[256,512]{1,0:T(8,128)(2,1)S(1)}, bf16[256,512]{1,0:T(8,128)(2,1)S(1)}, u32[]{:S(2)}, u32[]{:S(2)}) collective-permute-start(bf16[256,512]{1,0:T(8,128)(2,1)S(1)} %add_convert_fusion.1), channel_id=1, source_target_pairs={{0,2},{1,3},{2,4},{3,5},{4,6},{5,7},{6,0},{7,1},{8,10},{9,11},{10,... | collective-permute-start | bytes 786440 | tf_op jit(solution)/shard_map/scatter_out/ppermute | solution.py:86
  (1 other events, 2.2 us)
where the time goes:
time: 106 us; the launch traced here: 105 us
  waiting for transfers between devices  45.1 us (43%)
  starting transfers between devices  36.1 us (34%)
  Pallas kernels  18.1 us (17%)
  local copies, waits for them, and re-layouts  3.27 us (3%)
  other arithmetic  2.09 us (2%)
    ppermute x16, waiting for transfers between devices, send(): return lax.ppermute(rows, 'tp', tp_pairs(dx, flip))  23.3 us
    ppermute x16, starting transfers between devices, send(): return lax.ppermute(rows, 'tp', tp_pairs(dx, flip))  23.3 us
    pallas_call x8, Pallas kernels, attend(): call(lambda *refs: attend_kernel(index, side, *refs), sent_shapes if send...  11.5 us
    ppermute x1, waiting for transfers between devices, body(): column = jnp.concatenate([kv, lax.ppermute(kv, 'ctx', FLIP_Y)], axis=0)  6.75 us
    ppermute x1, waiting for transfers between devices, body(): lax.ppermute(column, 'ctx', UP_Z)  5.86 us
    ppermute x1, starting transfers between devices, body(): lax.ppermute(up2, 'ctx', UP_Z)  2.96 us
    ppermute x1, waiting for transfers between devices, body(): lax.ppermute(down2, 'ctx', DOWN_Z)  2.59 us
    ppermute x1, starting transfers between devices, body(): lax.ppermute(down, 'ctx', DOWN_Z)  2.31 us
  transfers between devices with their start and end apart: 28, of which 18 were waited for; matrix products, arithmetic and copies ran while one was open for 4% of the time, Pallas kernels for 13%

commit v1 on v0

--- a/solution.py
+++ b/solution.py
@@ -37,7 +37,7 @@
     [(-3, 0), (-3, 1), (3, 0), (3, 1)],
     [(4, 0), (4, 1)],
 ]
-NARROW = [4, 4, 4, 2]
+NARROW = [4, 4, 4, 4]
 FIRST_SLOT = [0]
 for chunk in CHUNKS:
     FIRST_SLOT.append(FIRST_SLOT[-1] + OWN_BLOCKS * len(chunk))
@@ -155,7 +155,7 @@
             which = c * QUERY_BLOCKS + b
             n = count_sc[which]
             meta_out[2 * which] = n
-            for g in range(NARROW[c] - 1):
+            for g in range(NARROW[c]):
                 slot_out[which * LIST + n + g] = 0
                 pos_out[which * LIST + n + g] = BLOCKS
 
@@ -273,12 +273,19 @@
             step(which * LIST + done + i * narrow_width, narrow_width, True)
             return carry
 
+        if index == len(CHUNKS) - 1:
+            step(which * LIST, narrow_width, True)
+            return unused
         if has_wide:
             lax.fori_loop(0, plain // WIDE, wide, 0)
         lax.fori_loop(0, (count - done + narrow_width - 1) // narrow_width, narrow, 0)
         return unused
 
-    lax.fori_loop(0, OWN_BLOCKS, block, 0)
+    if index == len(CHUNKS) - 1:
+        for b in range(OWN_BLOCKS):
+            block(b, 0)
+    else:
+        lax.fori_loop(0, OWN_BLOCKS, block, 0)
     if sends:
         rows_ref, stats_ref = refs[2:4]
         for b in range(OWN_BLOCKS):

time: 106 us -> 105 us (level)
  the two profiles are of different devices: /device:TPU:48 before, /device:TPU:96 now
where the time goes in v1:
time: 105 us; the launch traced here: 104 us
  starting transfers between devices  37.7 us (36%)
  waiting for transfers between devices  36.6 us (35%)
  Pallas kernels  23.5 us (22%)
  local copies, waits for them, and re-layouts  3.23 us (3%)
  other arithmetic  2.09 us (2%)
    ppermute x16, starting transfers between devices, send(): return lax.ppermute(rows, 'tp', tp_pairs(dx, flip))  22.7 us
    ppermute x16, waiting for transfers between devices, send(): return lax.ppermute(rows, 'tp', tp_pairs(dx, flip))  22.4 us
    pallas_call x8, Pallas kernels, attend(): call(lambda *refs: attend_kernel(index, side, *refs), sent_shapes if send...  16.5 us
    ppermute x1, waiting for transfers between devices, body(): lax.ppermute(column, 'ctx', UP_Z)  5.4 us
    ppermute x1, waiting for transfers between devices, body(): column = jnp.concatenate([kv, lax.ppermute(kv, 'ctx', FLIP_Y)], axis=0)  4.14 us
    ppermute x1, starting transfers between devices, body(): lax.ppermute(up, 'ctx', UP_Z)  3.69 us
    ppermute x1, starting transfers between devices, body(): column = jnp.concatenate([kv, lax.ppermute(kv, 'ctx', FLIP_Y)], axis=0)  3.55 us
    ppermute x1, waiting for transfers between devices, body(): lax.ppermute(down, 'ctx', DOWN_Z)  3.25 us
  transfers between devices with their start and end apart: 28, of which 15 were waited for; matrix products, arithmetic and copies ran while one was open for 4% of the time, Pallas kernels for 18%

profile of v1, /device:TPU:96, one launch (start us, length us, event | category | flops | bytes accessed | tf_op | source)
XLA Modules:
  0.0 103.6 jit_solution(8601726838155843122)
XLA Ops:
  0.0 1.6 %collective-permute-start = (bf16[256,512]{1,0:T(8,128)(2,1)}, bf16[256,512]{1,0:T(8,128)(2,1)S(1)}, u32[]{:S(2)}, u32[]{:S(2)}) collective-permute-start(bf16[256,512]{1,0:T(8,128)(2,1)} %refs_0_.1), channel_id=1, source_target_pairs={{0,1},{1,0},{2,3},{3,2},{4,5},{5,4},{6,7},{7,6},{8,9},{9,8},{10,11... | collective-permute-start | bytes 786440 | tf_op jit(solution)/shard_map/gather_hidden/ppermute | solution.py:86
  1.6 1.5 %collective-permute-start.1 = (bf16[256,512]{1,0:T(8,128)(2,1)}, bf16[256,512]{1,0:T(8,128)(2,1)S(1)}, u32[]{:S(2)}, u32[]{:S(2)}) collective-permute-start(bf16[256,512]{1,0:T(8,128)(2,1)} %refs_0_.1), channel_id=1, source_target_pairs={{0,2},{1,3},{2,4},{3,5},{4,6},{5,7},{6,0},{7,1},{8,10},{9,11},{10,... | collective-permute-start | bytes 786440 | tf_op jit(solution)/shard_map/gather_hidden/ppermute | solution.py:86
  3.1 1.7 %collective-permute-start.2 = (bf16[256,512]{1,0:T(8,128)(2,1)}, bf16[256,512]{1,0:T(8,128)(2,1)S(1)}, u32[]{:S(2)}, u32[]{:S(2)}) collective-permute-start(bf16[256,512]{1,0:T(8,128)(2,1)} %refs_0_.1), channel_id=1, source_target_pairs={{0,6},{1,7},{2,0},{3,1},{4,2},{5,3},{6,4},{7,5},{8,14},{9,15},{10,... | collective-permute-start | bytes 786440 | tf_op jit(solution)/shard_map/gather_hidden/ppermute | solution.py:86
  7.9 2.6 %shard_map.74 = (s32[512]{0:T(512)S(1)}, s32[512]{0:T(512)S(1)}, s32[37]{0:T(128)S(1)}) custom-call(s32[64]{0:T(128)S(1)} %copy-done.3, s32[4]{0:T(128)S(1)} %copy-done.4, s32[1]{0:T(128)} %bitcast.1.ctx_ref), custom_call_target="tpu_custom_call" | custom-call | bytes 4194304 | tf_op jit(solution)/shard_map/pallas_call | solution.py:380
  11.3 3.0 %collective-permute-start.4 = (bf16[256,512]{1,0:T(8,128)(2,1)S(1)}, bf16[256,512]{1,0:T(8,128)(2,1)S(1)}, u32[]{:S(2)}, u32[]{:S(2)}) collective-permute-start(bf16[256,512]{1,0:T(8,128)(2,1)S(1)} %pad_maximum_fusion.1), channel_id=1, source_target_pairs={{0,6},{1,7},{2,0},{3,1},{4,2},{5,3},{6,4},{7,5},{8,14},{9,15},{10,... | collective-permute-start | bytes 786440 | tf_op jit(solution)/shard_map/gather_hidden/ppermute | solution.py:86
  15.4 3.7 %collective-permute-done.3.refs_4_.a = bf16[256,512]{1,0:T(8,128)(2,1)S(1)} collective-permute-done((bf16[256,512]{1,0:T(8,128)(2,1)S(1)}, bf16[256,512]{1,0:T(8,128)(2,1)S(1)}, u32[]{:S(2)}, u32[]{:S(2)}) %collective-permute-start.3) | collective-permute-done | bytes 262176 | tf_op jit(solution)/shard_map/gather_hidden/ppermute | solution.py:86
  19.3 3.3 %collective-permute-start.7 = (bf16[128,512]{1,0:T(8,128)(2,1)S(1)}, bf16[128,512]{1,0:T(8,128)(2,1)S(1)}, u32[]{:S(2)}, u32[]{:S(2)}) collective-permute-start(bf16[128,512]{1,0:T(8,128)(2,1)S(1)} %slice.79), channel_id=1, source_target_pairs={{0,6},{1,7},{2,0},{3,1},{4,2},{5,3},{6,4},{7,5},{8,14},{9,15},{10,... | collective-permute-start | bytes 393224 | tf_op jit(solution)/shard_map/gather_hidden/ppermute | solution.py:86
  23.2 2.2 %collective-permute-done.6.refs_7_.d = bf16[128,512]{1,0:T(8,128)(2,1)S(1)} collective-permute-done((bf16[128,512]{1,0:T(8,128)(2,1)S(1)}, bf16[128,512]{1,0:T(8,128)(2,1)S(1)}, u32[]{:S(2)}, u32[]{:S(2)}) %collective-permute-start.6) | collective-permute-done | bytes 131104 | tf_op jit(solution)/shard_map/gather_hidden/ppermute | solution.py:86
  27.4 3.5 %collective-permute-start.8 = (bf16[256,256]{1,0:T(8,128)(2,1)S(1)}, bf16[256,256]{1,0:T(8,128)(2,1)S(1)}, u32[]{:S(2)}, u32[]{:S(2)}) collective-permute-start(bf16[256,256]{1,0:T(8,128)(2,1)S(1)} %shard_map.76), channel_id=1, source_target_pairs={{0,16},{8,24},{16,0},{24,8},{32,48},{40,56},{48,32},{56,40},{64,80... | collective-permute-start | bytes 393224 | tf_op jit(solution)/shard_map/gather_kv/ppermute | solution.py:437
  31.0 4.1 %collective-permute-done.8 = bf16[256,256]{1,0:T(8,128)(2,1)S(1)} collective-permute-done((bf16[256,256]{1,0:T(8,128)(2,1)S(1)}, bf16[256,256]{1,0:T(8,128)(2,1)S(1)}, u32[]{:S(2)}, u32[]{:S(2)}) %collective-permute-start.8) | collective-permute-done | bytes 131104 | tf_op jit(solution)/shard_map/gather_kv/ppermute | solution.py:437
  35.2 2.9 %collective-permute-start.10 = (bf16[512,256]{1,0:T(8,128)(2,1)S(1)}, bf16[512,256]{1,0:T(8,128)(2,1)S(1)}, u32[]{:S(2)}, u32[]{:S(2)}) collective-permute-start(bf16[512,256]{1,0:T(8,128)(2,1)S(1)} %pad_maximum_fusion.3), channel_id=1, source_target_pairs={{0,32},{8,40},{16,48},{24,56},{32,64},{40,72},{48,80},{56,88},{64,... | collective-permute-start | bytes 786440 | tf_op jit(solution)/shard_map/gather_kv/ppermute | solution.py:439
  38.0 5.4 %collective-permute-done.10 = bf16[512,256]{1,0:T(8,128)(2,1)S(1)} collective-permute-done((bf16[512,256]{1,0:T(8,128)(2,1)S(1)}, bf16[512,256]{1,0:T(8,128)(2,1)S(1)}, u32[]{:S(2)}, u32[]{:S(2)}) %collective-permute-start.10) | collective-permute-done | bytes 262176 | tf_op jit(solution)/shard_map/gather_kv/ppermute | solution.py:439
  43.4 3.7 %collective-permute-start.11 = (bf16[512,256]{1,0:T(8,128)(2,1)S(1)}, bf16[512,256]{1,0:T(8,128)(2,1)S(1)}, u32[]{:S(2)}, u32[]{:S(2)}) collective-permute-start(bf16[512,256]{1,0:T(8,128)(2,1)S(1)} %collective-permute-done.10), channel_id=1, source_target_pairs={{0,32},{8,40},{16,48},{24,56},{32,64},{40,72},{48,80},{56,88},{64,... | collective-permute-start | bytes 786440 | tf_op jit(solution)/shard_map/gather_kv/ppermute | solution.py:440
  47.2 2.0 %gather_kv.10 = (f32[2,512,128]{2,1,0:T(8,128)S(1)}, f32[2,512,256]{2,1,0:T(8,128)S(1)}) custom-call(s32[512]{0:T(512)S(1)} %get-tuple-element.64.refs_0_, s32[512]{0:T(512)S(1)} %get-tuple-element.65.refs_1_, s32[37]{0:T(128)S(1)} %get-tuple-element.66.refs_2_, bf16[2,512,128]{2,1,0:T(8,128)(2,1)S(1)} %shard_map.75.refs_3_, ...), custom_call_target="tpu_custom_call" | custom-call | flops 402653184 | bytes 4194304 | tf_op jit(solution)/shard_map/gather_kv/pallas_call | solution.py:425
  49.2 2.6 %gather_kv.9 = (f32[2,512,128]{2,1,0:T(8,128)S(1)}, f32[2,512,256]{2,1,0:T(8,128)S(1)}) custom-call(s32[512]{0:T(512)S(1)} %get-tuple-element.64.refs_0_, s32[512]{0:T(512)S(1)} %get-tuple-element.65.refs_1_, s32[37]{0:T(128)S(1)} %get-tuple-element.66.refs_2_, bf16[2,512,128]{2,1,0:T(8,128)(2,1)S(1)} %collective-permute-done.9.refs_3_, ...), custom_call_target="tpu_custom_call" | custom-call | flops 402653184 | bytes 4194304 | tf_op jit(solution)/shard_map/gather_kv/pallas_call | solution.py:425
  51.8 3.3 %collective-permute-done.13 = bf16[512,256]{1,0:T(8,128)(2,1)S(1)} collective-permute-done((bf16[512,256]{1,0:T(8,128)(2,1)S(1)}, bf16[512,256]{1,0:T(8,128)(2,1)S(1)}, u32[]{:S(2)}, u32[]{:S(2)}) %collective-permute-start.13) | collective-permute-done | bytes 262176 | tf_op jit(solution)/shard_map/gather_kv/ppermute | solution.py:440
  55.4 1.7 %collective-permute-start.15 = (bf16[512,256]{1,0:T(8,128)(2,1)S(1)}, bf16[512,256]{1,0:T(8,128)(2,1)S(1)}, u32[]{:S(2)}, u32[]{:S(2)}) collective-permute-start(bf16[512,256]{1,0:T(8,128)(2,1)S(1)} %collective-permute-done.13), channel_id=1, source_target_pairs={{0,224},{8,232},{16,240},{24,248},{32,0},{40,8},{48,16},{56,24},{6... | collective-permute-start | bytes 786440 | tf_op jit(solution)/shard_map/gather_kv/ppermute | solution.py:444
  57.2 2.0 %gather_kv.12 = (f32[2,512,128]{2,1,0:T(8,128)S(1)}, f32[2,512,256]{2,1,0:T(8,128)S(1)}) custom-call(s32[512]{0:T(512)S(1)} %get-tuple-element.64.refs_0_, s32[512]{0:T(512)S(1)} %get-tuple-element.65.refs_1_, s32[37]{0:T(128)S(1)} %get-tuple-element.66.refs_2_, bf16[2,512,128]{2,1,0:T(8,128)(2,1)S(1)} %shard_map.75.refs_3_, ...), custom_call_target="tpu_custom_call" | custom-call | flops 268435456 | bytes 4194304 | tf_op jit(solution)/shard_map/gather_kv/pallas_call | solution.py:425
  59.1 2.6 %gather_kv.11 = (f32[2,512,128]{2,1,0:T(8,128)S(1)}, f32[2,512,256]{2,1,0:T(8,128)S(1)}) custom-call(s32[512]{0:T(512)S(1)} %get-tuple-element.64.refs_0_, s32[512]{0:T(512)S(1)} %get-tuple-element.65.refs_1_, s32[37]{0:T(128)S(1)} %get-tuple-element.66.refs_2_, bf16[2,512,128]{2,1,0:T(8,128)(2,1)S(1)} %collective-permute-done.9.refs_3_, ...), custom_call_target="tpu_custom_call" | custom-call | flops 268435456 | bytes 4194304 | tf_op jit(solution)/shard_map/gather_kv/pallas_call | solution.py:425
  63.1 2.1 %collective-permute-start.17 = (bf16[256,256]{1,0:T(8,128)(2,1)S(1)}, bf16[256,256]{1,0:T(8,128)(2,1)S(1)}, u32[]{:S(2)}, u32[]{:S(2)}) collective-permute-start(bf16[256,256]{1,0:T(8,128)(2,1)S(1)} %slice.63), channel_id=1, source_target_pairs={{0,224},{8,232},{16,240},{24,248},{32,0},{40,8},{48,16},{56,24},{6... | collective-permute-start | bytes 393224 | tf_op jit(solution)/shard_map/gather_kv/ppermute | solution.py:448
  65.2 2.0 %gather_kv.14 = (f32[2,512,128]{2,1,0:T(8,128)S(1)}, f32[2,512,256]{2,1,0:T(8,128)S(1)}) custom-call(s32[512]{0:T(512)S(1)} %get-tuple-element.64.refs_0_, s32[512]{0:T(512)S(1)} %get-tuple-element.65.refs_1_, s32[37]{0:T(128)S(1)} %get-tuple-element.66.refs_2_, bf16[2,512,128]{2,1,0:T(8,128)(2,1)S(1)} %shard_map.75.refs_3_, ...), custom_call_target="tpu_custom_call" | custom-call | flops 268435456 | bytes 4194304 | tf_op jit(solution)/shard_map/gather_kv/pallas_call | solution.py:425
  67.2 2.0 %gather_kv.13 = (f32[2,512,128]{2,1,0:T(8,128)S(1)}, f32[2,512,256]{2,1,0:T(8,128)S(1)}) custom-call(s32[512]{0:T(512)S(1)} %get-tuple-element.64.refs_0_, s32[512]{0:T(512)S(1)} %get-tuple-element.65.refs_1_, s32[37]{0:T(128)S(1)} %get-tuple-element.66.refs_2_, bf16[2,512,128]{2,1,0:T(8,128)(2,1)S(1)} %collective-permute-done.9.refs_3_, ...), custom_call_target="tpu_custom_call" | custom-call | flops 268435456 | bytes 4194304 | tf_op jit(solution)/shard_map/gather_kv/pallas_call | solution.py:425
  69.4 1.7 %gather_kv.16 = (bf16[2,512,128]{2,1,0:T(8,128)(2,1)S(1)}, f32[16,128]{1,0:T(8,128)S(1)}) custom-call(s32[512]{0:T(512)S(1)} %get-tuple-element.64.refs_0_, s32[512]{0:T(512)S(1)} %get-tuple-element.65.refs_1_, s32[37]{0:T(128)S(1)} %get-tuple-element.66.refs_2_, bf16[2,512,128]{2,1,0:T(8,128)(2,1)S(1)} %collective-permute-done.9.refs_3_, ...), custom_call_target="tpu_custom_call" | custom-call | flops 134217728 | bytes 4194304 | tf_op jit(solution)/shard_map/gather_kv/pallas_call | solution.py:425
  71.7 1.7 %gather_kv.15 = (f32[2,512,128]{2,1,0:T(8,128)S(1)}, f32[2,512,256]{2,1,0:T(8,128)S(1)}) custom-call(s32[512]{0:T(512)S(1)} %get-tuple-element.64.refs_0_, s32[512]{0:T(512)S(1)} %get-tuple-element.65.refs_1_, s32[37]{0:T(128)S(1)} %get-tuple-element.66.refs_2_, bf16[2,512,128]{2,1,0:T(8,128)(2,1)S(1)} %shard_map.75.refs_3_, ...), custom_call_target="tpu_custom_call" | custom-call | flops 134217728 | bytes 4194304 | tf_op jit(solution)/shard_map/gather_kv/pallas_call | solution.py:425
  74.7 3.4 %collective-permute-start.20 = (bf16[128,512]{1,0:T(8,128)(2,1)S(1)}, bf16[128,512]{1,0:T(8,128)(2,1)S(1)}, u32[]{:S(2)}, u32[]{:S(2)}) collective-permute-start(bf16[128,512]{1,0:T(8,128)(2,1)S(1)} %get-tuple-element.110), channel_id=1, source_target_pairs={{0,6},{1,7},{2,0},{3,1},{4,2},{5,3},{6,4},{7,5},{8,14},{9,15},{10,... | collective-permute-start | bytes 393224 | tf_op jit(solution)/shard_map/scatter_out/ppermute | solution.py:86
  79.5 1.9 %collective-permute-done.20 = bf16[128,512]{1,0:T(8,128)(2,1)S(1)} collective-permute-done((bf16[128,512]{1,0:T(8,128)(2,1)S(1)}, bf16[128,512]{1,0:T(8,128)(2,1)S(1)}, u32[]{:S(2)}, u32[]{:S(2)}) %collective-permute-start.20) | collective-permute-done | bytes 131104 | tf_op jit(solution)/shard_map/scatter_out/ppermute | solution.py:86
  81.5 3.8 %collective-permute-start.21 = (bf16[256,512]{1,0:T(8,128)(2,1)S(1)}, bf16[256,512]{1,0:T(8,128)(2,1)S(1)}, u32[]{:S(2)}, u32[]{:S(2)}) collective-permute-start(bf16[256,512]{1,0:T(8,128)(2,1)S(1)} %pad_maximum_fusion.4), channel_id=1, source_target_pairs={{0,6},{1,7},{2,0},{3,1},{4,2},{5,3},{6,4},{7,5},{8,14},{9,15},{10,... | collective-permute-start | bytes 786440 | tf_op jit(solution)/shard_map/scatter_out/ppermute | solution.py:86
  86.6 3.9 %collective-permute-done.21 = bf16[256,512]{1,0:T(8,128)(2,1)S(1)} collective-permute-done((bf16[256,512]{1,0:T(8,128)(2,1)S(1)}, bf16[256,512]{1,0:T(8,128)(2,1)S(1)}, u32[]{:S(2)}, u32[]{:S(2)}) %collective-permute-start.21) | collective-permute-done | bytes 262176 | tf_op jit(solution)/shard_map/scatter_out/ppermute | solution.py:86
  90.5 3.5 %collective-permute-done.23 = bf16[256,512]{1,0:T(8,128)(2,1)S(1)} collective-permute-done((bf16[256,512]{1,0:T(8,128)(2,1)S(1)}, bf16[256,512]{1,0:T(8,128)(2,1)S(1)}, u32[]{:S(2)}, u32[]{:S(2)}) %collective-permute-start.23) | collective-permute-done | bytes 262176 | tf_op jit(solution)/shard_map/scatter_out/ppermute | solution.py:86
  95.1 1.9 %collective-permute-start.27 = (bf16[256,512]{1,0:T(8,128)(2,1)S(1)}, bf16[256,512]{1,0:T(8,128)(2,1)S(1)}, u32[]{:S(2)}, u32[]{:S(2)}) collective-permute-start(bf16[256,512]{1,0:T(8,128)(2,1)S(1)} %add_convert_fusion.1), channel_id=1, source_target_pairs={{0,2},{1,3},{2,4},{3,5},{4,6},{5,7},{6,0},{7,1},{8,10},{9,11},{10,... | collective-permute-start | bytes 786440 | tf_op jit(solution)/shard_map/scatter_out/ppermute | solution.py:86
  97.0 3.7 %collective-permute-done.24 = bf16[256,512]{1,0:T(8,128)(2,1)S(1)} collective-permute-done((bf16[256,512]{1,0:T(8,128)(2,1)S(1)}, bf16[256,512]{1,0:T(8,128)(2,1)S(1)}, u32[]{:S(2)}, u32[]{:S(2)}) %collective-permute-start.24) | collective-permute-done | bytes 262176 | tf_op jit(solution)/shard_map/scatter_out/ppermute | solution.py:86
  101.2 1.5 %collective-permute-done.27 = bf16[256,512]{1,0:T(8,128)(2,1)S(1)} collective-permute-done((bf16[256,512]{1,0:T(8,128)(2,1)S(1)}, bf16[256,512]{1,0:T(8,128)(2,1)S(1)}, u32[]{:S(2)}, u32[]{:S(2)}) %collective-permute-start.27) | collective-permute-done | bytes 262176 | tf_op jit(solution)/shard_map/scatter_out/ppermute | solution.py:86
  (89 shorter events, 16.5 us)
Async XLA Ops:
  0.0 6.2 %copy-start.3 = (s32[64]{0:T(128)S(1)}, s32[64]{0:T(128)}, u32[]{:S(2)}) copy-start(s32[64]{0:T(128)} %span_ref.1) | copy-start | bytes 772
  0.0 10.8 %collective-permute-start = (bf16[256,512]{1,0:T(8,128)(2,1)}, bf16[256,512]{1,0:T(8,128)(2,1)S(1)}, u32[]{:S(2)}, u32[]{:S(2)}) collective-permute-start(bf16[256,512]{1,0:T(8,128)(2,1)} %refs_0_.1), channel_id=1, source_target_pairs={{0,1},{1,0},{2,3},{3,2},{4,5},{5,4},{6,7},{7,6},{8,9},{9,8},{10,11... | collective-permute-start | bytes 786440 | tf_op jit(solution)/shard_map/gather_hidden/ppermute | solution.py:86
  1.6 9.2 %collective-permute-start.1 = (bf16[256,512]{1,0:T(8,128)(2,1)}, bf16[256,512]{1,0:T(8,128)(2,1)S(1)}, u32[]{:S(2)}, u32[]{:S(2)}) collective-permute-start(bf16[256,512]{1,0:T(8,128)(2,1)} %refs_0_.1), channel_id=1, source_target_pairs={{0,2},{1,3},{2,4},{3,5},{4,6},{5,7},{6,0},{7,1},{8,10},{9,11},{10,... | collective-permute-start | bytes 786440 | tf_op jit(solution)/shard_map/gather_hidden/ppermute | solution.py:86
  3.1 8.2 %collective-permute-start.2 = (bf16[256,512]{1,0:T(8,128)(2,1)}, bf16[256,512]{1,0:T(8,128)(2,1)S(1)}, u32[]{:S(2)}, u32[]{:S(2)}) collective-permute-start(bf16[256,512]{1,0:T(8,128)(2,1)} %refs_0_.1), channel_id=1, source_target_pairs={{0,6},{1,7},{2,0},{3,1},{4,2},{5,3},{6,4},{7,5},{8,14},{9,15},{10,... | collective-permute-start | bytes 786440 | tf_op jit(solution)/shard_map/gather_hidden/ppermute | solution.py:86
  4.8 3.1 %copy-start.4 = (s32[4]{0:T(128)S(1)}, s32[4]{0:T(128)}, u32[]{:S(2)}) copy-start(s32[4]{0:T(128)} %len_ref.1) | copy-start | bytes 52
  10.8 11.9 %copy-start.2 = (bf16[256,512]{1,0:T(8,128)(2,1)S(1)}, bf16[256,512]{1,0:T(8,128)(2,1)}, u32[]{:S(2)}) copy-start(bf16[256,512]{1,0:T(8,128)(2,1)} %refs_0_.1) | copy-start | bytes 786436
  10.9 8.3 %collective-permute-start.3 = (bf16[256,512]{1,0:T(8,128)(2,1)S(1)}, bf16[256,512]{1,0:T(8,128)(2,1)S(1)}, u32[]{:S(2)}, u32[]{:S(2)}) collective-permute-start(bf16[256,512]{1,0:T(8,128)(2,1)S(1)} %pad_maximum_fusion), channel_id=1, source_target_pairs={{0,2},{1,3},{2,4},{3,5},{4,6},{5,7},{6,0},{7,1},{8,10},{9,11},{10,... | collective-permute-start | bytes 786440 | tf_op jit(solution)/shard_map/gather_hidden/ppermute | solution.py:86
  11.3 8.0 %collective-permute-start.4 = (bf16[256,512]{1,0:T(8,128)(2,1)S(1)}, bf16[256,512]{1,0:T(8,128)(2,1)S(1)}, u32[]{:S(2)}, u32[]{:S(2)}) collective-permute-start(bf16[256,512]{1,0:T(8,128)(2,1)S(1)} %pad_maximum_fusion.1), channel_id=1, source_target_pairs={{0,6},{1,7},{2,0},{3,1},{4,2},{5,3},{6,4},{7,5},{8,14},{9,15},{10,... | collective-permute-start | bytes 786440 | tf_op jit(solution)/shard_map/gather_hidden/ppermute | solution.py:86
  14.3 8.8 %collective-permute-start.5 = (bf16[256,512]{1,0:T(8,128)(2,1)S(1)}, bf16[256,512]{1,0:T(8,128)(2,1)S(1)}, u32[]{:S(2)}, u32[]{:S(2)}) collective-permute-start(bf16[256,512]{1,0:T(8,128)(2,1)S(1)} %pad_maximum_fusion.2), channel_id=1, source_target_pairs={{0,1},{1,0},{2,3},{3,2},{4,5},{5,4},{6,7},{7,6},{8,9},{9,8},{10,11... | collective-permute-start | bytes 786440 | tf_op jit(solution)/shard_map/gather_hidden/ppermute | solution.py:86
  19.1 6.3 %collective-permute-start.6 = (bf16[128,512]{1,0:T(8,128)(2,1)S(1)}, bf16[128,512]{1,0:T(8,128)(2,1)S(1)}, u32[]{:S(2)}, u32[]{:S(2)}) collective-permute-start(bf16[128,512]{1,0:T(8,128)(2,1)S(1)} %slice.78), channel_id=1, source_target_pairs={{0,2},{1,3},{2,4},{3,5},{4,6},{5,7},{6,0},{7,1},{8,10},{9,11},{10,... | collective-permute-start | bytes 393224 | tf_op jit(solution)/shard_map/gather_hidden/ppermute | solution.py:86
  19.2 6.2 %copy-start.1 = (bf16[4096,512]{1,0:T(8,128)(2,1)S(1)}, bf16[4096,512]{1,0:T(8,128)(2,1)}, u32[]{:S(2)}) copy-start(bf16[4096,512]{1,0:T(8,128)(2,1)} %refs_9_.1) | copy-start | bytes 12582916
  19.3 6.1 %collective-permute-start.7 = (bf16[128,512]{1,0:T(8,128)(2,1)S(1)}, bf16[128,512]{1,0:T(8,128)(2,1)S(1)}, u32[]{:S(2)}, u32[]{:S(2)}) collective-permute-start(bf16[128,512]{1,0:T(8,128)(2,1)S(1)} %slice.79), channel_id=1, source_target_pairs={{0,6},{1,7},{2,0},{3,1},{4,2},{5,3},{6,4},{7,5},{8,14},{9,15},{10,... | collective-permute-start | bytes 393224 | tf_op jit(solution)/shard_map/gather_hidden/ppermute | solution.py:86
  26.8 8.3 %collective-permute-start.9 = (bf16[2,512,128]{2,1,0:T(8,128)(2,1)S(1)}, bf16[2,512,128]{2,1,0:T(8,128)(2,1)S(1)}, u32[]{:S(2)}, u32[]{:S(2)}) collective-permute-start(bf16[2,512,128]{2,1,0:T(8,128)(2,1)S(1)} %shard_map.75.refs_3_), channel_id=1, source_target_pairs={{0,8},{8,0},{16,24},{24,16},{32,40},{40,32},{48,56},{56,48},{64,72... | collective-permute-start | bytes 786440 | tf_op jit(solution)/shard_map/gather_kv/ppermute | solution.py:436
  27.4 7.7 %collective-permute-start.8 = (bf16[256,256]{1,0:T(8,128)(2,1)S(1)}, bf16[256,256]{1,0:T(8,128)(2,1)S(1)}, u32[]{:S(2)}, u32[]{:S(2)}) collective-permute-start(bf16[256,256]{1,0:T(8,128)(2,1)S(1)} %shard_map.76), channel_id=1, source_target_pairs={{0,16},{8,24},{16,0},{24,8},{32,48},{40,56},{48,32},{56,40},{64,80... | collective-permute-start | bytes 393224 | tf_op jit(solution)/shard_map/gather_kv/ppermute | solution.py:437
  35.2 8.3 %collective-permute-start.10 = (bf16[512,256]{1,0:T(8,128)(2,1)S(1)}, bf16[512,256]{1,0:T(8,128)(2,1)S(1)}, u32[]{:S(2)}, u32[]{:S(2)}) collective-permute-start(bf16[512,256]{1,0:T(8,128)(2,1)S(1)} %pad_maximum_fusion.3), channel_id=1, source_target_pairs={{0,32},{8,40},{16,48},{24,56},{32,64},{40,72},{48,80},{56,88},{64,... | collective-permute-start | bytes 786440 | tf_op jit(solution)/shard_map/gather_kv/ppermute | solution.py:439
  38.0 9.1 %collective-permute-start.12 = (bf16[512,256]{1,0:T(8,128)(2,1)S(1)}, bf16[512,256]{1,0:T(8,128)(2,1)S(1)}, u32[]{:S(2)}, u32[]{:S(2)}) collective-permute-start(bf16[512,256]{1,0:T(8,128)(2,1)S(1)} %pad_maximum_fusion.3), channel_id=1, source_target_pairs={{0,224},{8,232},{16,240},{24,248},{32,0},{40,8},{48,16},{56,24},{6... | collective-permute-start | bytes 786440 | tf_op jit(solution)/shard_map/gather_kv/ppermute | solution.py:439
  43.4 8.4 %collective-permute-start.11 = (bf16[512,256]{1,0:T(8,128)(2,1)S(1)}, bf16[512,256]{1,0:T(8,128)(2,1)S(1)}, u32[]{:S(2)}, u32[]{:S(2)}) collective-permute-start(bf16[512,256]{1,0:T(8,128)(2,1)S(1)} %collective-permute-done.10), channel_id=1, source_target_pairs={{0,32},{8,40},{16,48},{24,56},{32,64},{40,72},{48,80},{56,88},{64,... | collective-permute-start | bytes 786440 | tf_op jit(solution)/shard_map/gather_kv/ppermute | solution.py:440
  47.1 7.9 %collective-permute-start.13 = (bf16[512,256]{1,0:T(8,128)(2,1)S(1)}, bf16[512,256]{1,0:T(8,128)(2,1)S(1)}, u32[]{:S(2)}, u32[]{:S(2)}) collective-permute-start(bf16[512,256]{1,0:T(8,128)(2,1)S(1)} %collective-permute-done.12), channel_id=1, source_target_pairs={{0,224},{8,232},{16,240},{24,248},{32,0},{40,8},{48,16},{56,24},{6... | collective-permute-start | bytes 786440 | tf_op jit(solution)/shard_map/gather_kv/ppermute | solution.py:440
  55.1 6.7 %collective-permute-start.14 = (bf16[512,256]{1,0:T(8,128)(2,1)S(1)}, bf16[512,256]{1,0:T(8,128)(2,1)S(1)}, u32[]{:S(2)}, u32[]{:S(2)}) collective-permute-start(bf16[512,256]{1,0:T(8,128)(2,1)S(1)} %collective-permute-done.11), channel_id=1, source_target_pairs={{0,32},{8,40},{16,48},{24,56},{32,64},{40,72},{48,80},{56,88},{64,... | collective-permute-start | bytes 786440 | tf_op jit(solution)/shard_map/gather_kv/ppermute | solution.py:444
  55.4 7.6 %collective-permute-start.15 = (bf16[512,256]{1,0:T(8,128)(2,1)S(1)}, bf16[512,256]{1,0:T(8,128)(2,1)S(1)}, u32[]{:S(2)}, u32[]{:S(2)}) collective-permute-start(bf16[512,256]{1,0:T(8,128)(2,1)S(1)} %collective-permute-done.13), channel_id=1, source_target_pairs={{0,224},{8,232},{16,240},{24,248},{32,0},{40,8},{48,16},{56,24},{6... | collective-permute-start | bytes 786440 | tf_op jit(solution)/shard_map/gather_kv/ppermute | solution.py:444
  63.0 6.2 %collective-permute-start.16 = (bf16[256,256]{1,0:T(8,128)(2,1)S(1)}, bf16[256,256]{1,0:T(8,128)(2,1)S(1)}, u32[]{:S(2)}, u32[]{:S(2)}) collective-permute-start(bf16[256,256]{1,0:T(8,128)(2,1)S(1)} %slice.62), channel_id=1, source_target_pairs={{0,32},{8,40},{16,48},{24,56},{32,64},{40,72},{48,80},{56,88},{64,... | collective-permute-start | bytes 393224 | tf_op jit(solution)/shard_map/gather_kv/ppermute | solution.py:448
  63.1 6.3 %collective-permute-start.17 = (bf16[256,256]{1,0:T(8,128)(2,1)S(1)}, bf16[256,256]{1,0:T(8,128)(2,1)S(1)}, u32[]{:S(2)}, u32[]{:S(2)}) collective-permute-start(bf16[256,256]{1,0:T(8,128)(2,1)S(1)} %slice.63), channel_id=1, source_target_pairs={{0,224},{8,232},{16,240},{24,248},{32,0},{40,8},{48,16},{56,24},{6... | collective-permute-start | bytes 393224 | tf_op jit(solution)/shard_map/gather_kv/ppermute | solution.py:448
  71.1 2.3 %collective-permute-start.18 = (bf16[2,512,128]{2,1,0:T(8,128)(2,1)S(1)}, bf16[2,512,128]{2,1,0:T(8,128)(2,1)S(1)}, u32[]{:S(2)}, u32[]{:S(2)}) collective-permute-start(bf16[2,512,128]{2,1,0:T(8,128)(2,1)S(1)} %get-tuple-element.102), channel_id=1, source_target_pairs={{0,8},{8,0},{16,24},{24,16},{32,40},{40,32},{48,56},{56,48},{64,72... | collective-permute-start | bytes 786440 | tf_op jit(solution)/shard_map/gather_kv/ppermute | solution.py:453
  71.2 2.2 %collective-permute-start.19 = (f32[16,128]{1,0:T(8,128)S(1)}, f32[16,128]{1,0:T(8,128)S(1)}, u32[]{:S(2)}, u32[]{:S(2)}) collective-permute-start(f32[16,128]{1,0:T(8,128)S(1)} %get-tuple-element.103), channel_id=1, source_target_pairs={{0,8},{8,0},{16,24},{24,16},{32,40},{40,32},{48,56},{56,48},{64,72... | collective-permute-start | bytes 24584 | tf_op jit(solution)/shard_map/gather_kv/ppermute | solution.py:453
  74.7 6.7 %collective-permute-start.20 = (bf16[128,512]{1,0:T(8,128)(2,1)S(1)}, bf16[128,512]{1,0:T(8,128)(2,1)S(1)}, u32[]{:S(2)}, u32[]{:S(2)}) collective-permute-start(bf16[128,512]{1,0:T(8,128)(2,1)S(1)} %get-tuple-element.110), channel_id=1, source_target_pairs={{0,6},{1,7},{2,0},{3,1},{4,2},{5,3},{6,4},{7,5},{8,14},{9,15},{10,... | collective-permute-start | bytes 393224 | tf_op jit(solution)/shard_map/scatter_out/ppermute | solution.py:86
  78.2 7.1 %collective-permute-start.22 = (bf16[128,512]{1,0:T(8,128)(2,1)S(1)}, bf16[128,512]{1,0:T(8,128)(2,1)S(1)}, u32[]{:S(2)}, u32[]{:S(2)}) collective-permute-start(bf16[128,512]{1,0:T(8,128)(2,1)S(1)} %get-tuple-element.113), channel_id=1, source_target_pairs={{0,2},{1,3},{2,4},{3,5},{4,6},{5,7},{6,0},{7,1},{8,10},{9,11},{10,... | collective-permute-start | bytes 393224 | tf_op jit(solution)/shard_map/scatter_out/ppermute | solution.py:86
  78.3 8.3 %collective-permute-start.25 = (bf16[256,512]{1,0:T(8,128)(2,1)S(1)}, bf16[256,512]{1,0:T(8,128)(2,1)S(1)}, u32[]{:S(2)}, u32[]{:S(2)}) collective-permute-start(bf16[256,512]{1,0:T(8,128)(2,1)S(1)} %get-tuple-element.115), channel_id=1, source_target_pairs={{0,1},{1,0},{2,3},{3,2},{4,5},{5,4},{6,7},{7,6},{8,9},{9,8},{10,11... | collective-permute-start | bytes 786440 | tf_op jit(solution)/shard_map/scatter_out/ppermute | solution.py:86
  81.5 9.0 %collective-permute-start.21 = (bf16[256,512]{1,0:T(8,128)(2,1)S(1)}, bf16[256,512]{1,0:T(8,128)(2,1)S(1)}, u32[]{:S(2)}, u32[]{:S(2)}) collective-permute-start(bf16[256,512]{1,0:T(8,128)(2,1)S(1)} %pad_maximum_fusion.4), channel_id=1, source_target_pairs={{0,6},{1,7},{2,0},{3,1},{4,2},{5,3},{6,4},{7,5},{8,14},{9,15},{10,... | collective-permute-start | bytes 786440 | tf_op jit(solution)/shard_map/scatter_out/ppermute | solution.py:86
  85.3 8.7 %collective-permute-start.23 = (bf16[256,512]{1,0:T(8,128)(2,1)S(1)}, bf16[256,512]{1,0:T(8,128)(2,1)S(1)}, u32[]{:S(2)}, u32[]{:S(2)}) collective-permute-start(bf16[256,512]{1,0:T(8,128)(2,1)S(1)} %pad_maximum_fusion.5), channel_id=1, source_target_pairs={{0,2},{1,3},{2,4},{3,5},{4,6},{5,7},{6,0},{7,1},{8,10},{9,11},{10,... | collective-permute-start | bytes 786440 | tf_op jit(solution)/shard_map/scatter_out/ppermute | solution.py:86
  94.1 6.6 %collective-permute-start.24 = (bf16[256,512]{1,0:T(8,128)(2,1)S(1)}, bf16[256,512]{1,0:T(8,128)(2,1)S(1)}, u32[]{:S(2)}, u32[]{:S(2)}) collective-permute-start(bf16[256,512]{1,0:T(8,128)(2,1)S(1)} %add_convert_fusion.3), channel_id=1, source_target_pairs={{0,1},{1,0},{2,3},{3,2},{4,5},{5,4},{6,7},{7,6},{8,9},{9,8},{10,11... | collective-permute-start | bytes 786440 | tf_op jit(solution)/shard_map/scatter_out/ppermute | solution.py:86
  94.8 6.4 %collective-permute-start.26 = (bf16[256,512]{1,0:T(8,128)(2,1)S(1)}, bf16[256,512]{1,0:T(8,128)(2,1)S(1)}, u32[]{:S(2)}, u32[]{:S(2)}) collective-permute-start(bf16[256,512]{1,0:T(8,128)(2,1)S(1)} %add_convert_fusion.2), channel_id=1, source_target_pairs={{0,6},{1,7},{2,0},{3,1},{4,2},{5,3},{6,4},{7,5},{8,14},{9,15},{10,... | collective-permute-start | bytes 786440 | tf_op jit(solution)/shard_map/scatter_out/ppermute | solution.py:86
  95.1 7.7 %collective-permute-start.27 = (bf16[256,512]{1,0:T(8,128)(2,1)S(1)}, bf16[256,512]{1,0:T(8,128)(2,1)S(1)}, u32[]{:S(2)}, u32[]{:S(2)}) collective-permute-start(bf16[256,512]{1,0:T(8,128)(2,1)S(1)} %add_convert_fusion.1), channel_id=1, source_target_pairs={{0,2},{1,3},{2,4},{3,5},{4,6},{5,7},{6,0},{7,1},{8,10},{9,11},{10,... | collective-permute-start | bytes 786440 | tf_op jit(solution)/shard_map/scatter_out/ppermute | solution.py:86
  (1 other events, 2.6 us)
